TPU v7x, 32 devices: a whole 2x2x4 slice. The times are simulated.
32 devices in a mesh: dp: 8 (over z, y), mp: 4 (over x, core).
Axes of the slice: x: 2, y: 2, z: 4, core: 2. Of those that a mesh axis runs over, the one named last changes fastest.
Arguments:
- hidden_states: bfloat16 [4096, 3584], P('dp'), may hold values from -6 to 6
- token_ids: int32 [256, 16], P('dp'), may hold values from 0 to 152063, as said below
- norm_gain: float32 [3584], replicated, may hold values from 0.5 to 1.5
- q_weight: bfloat16 [3584, 3584], P('dp', 'mp'), may hold values from -0.09375 to 0.09375
- key_matrix: bfloat16 [3584, 512], P('dp', 'mp'), may hold values from -0.09375 to 0.09375
- value_matrix: bfloat16 [3584, 512], P('dp', 'mp'), may hold values from -0.09375 to 0.09375
- out_weight: bfloat16 [3584, 3584], P('dp', 'mp'), may hold values from -0.09375 to 0.09375
- label_table: bfloat16 [8192, 3584], P(('dp', 'mp')), may hold values from -6 to 6
- refresh_rows: int32 [256], P(('dp', 'mp')), may hold values from 0 to 255, as said below
- label_counts: int32 [8192], P(('dp', 'mp')), may hold values from 1 to 8191
- queries: bfloat16 [128, 3584], replicated, may hold values from -6 to 6
- positives: int32 [128, 8], replicated, may hold values from 0 to 8191
Outputs:
- label_grad: float32 [8192, 3584], P(('dp', 'mp'))
- query_grad: float32 [128, 3584], replicated
- loss: float32 [], replicated
Inputs may be any that keep to these rules, and one draw needn't show every extreme that they name: `token_ids`: in every text the first id is not 0, and after an id 0 all later ids of that text are 0. `refresh_rows`: the 8 entries of each aligned block of 8 entries are distinct.
All inputs are finite; a program needn't handle non-finite values.
Results may differ from a plain program's by a relative error of at most 0.003.
Values may be sent and summed in bfloat16 or wider, within the bound.
A program may use at most 128 MiB of HBM per device.

v0:
```python
import math

import jax
import jax.numpy as jnp
from jax import lax
from jax.sharding import PartitionSpec as P

HEAD_WIDTH = 128


rope_theta = 1000000.0
norm_eps = 1e-06
focal_beta = 0.9999


def rotary(values, head_size):
    length = values.shape[1]
    half = head_size // 2
    frequency = rope_theta ** (-2.0 * jnp.arange(half, dtype=jnp.float32) / head_size)
    angles = jnp.arange(length, dtype=jnp.float32)[:, None] * frequency[None, :]
    cosine = jnp.concatenate([jnp.cos(angles), jnp.cos(angles)], axis=1)[None, :, None, :]
    sine = jnp.concatenate([jnp.sin(angles), jnp.sin(angles)], axis=1)[None, :, None, :]
    turned = jnp.concatenate([-values[..., half:], values[..., :half]], axis=-1)
    return values * cosine + turned * sine


def attend(query_rows, key_rows, value_rows, text_ids, head_size):
    texts, length = text_ids.shape
    kv_heads = key_rows.shape[1] // head_size
    repeat = query_rows.shape[1] // head_size // kv_heads
    query_r = query_rows.reshape(texts, length, kv_heads, repeat, head_size)
    key_r = key_rows.reshape(texts, length, kv_heads, head_size)
    value_r = value_rows.reshape(texts, length, kv_heads, head_size)
    scores = jnp.einsum(
        "ntgrd,nsgd->ngrts", query_r, key_r, preferred_element_type=jnp.float32
    ) / math.sqrt(head_size)
    causal = jnp.arange(length)[:, None] >= jnp.arange(length)[None, :]
    allowed = causal[None, None, None, :, :] & (text_ids != 0)[:, None, None, None, :]
    weights = jnp.where(allowed, jnp.exp(scores), 0.0)
    probs = (weights / jnp.sum(weights, axis=-1, keepdims=True)).astype(jnp.bfloat16)
    mixed = jnp.einsum("ngrts,nsgd->ntgrd", probs, value_r, preferred_element_type=jnp.float32)
    return mixed.reshape(texts * length, -1).astype(jnp.bfloat16)


def shards(
    hidden_states,
    token_ids,
    norm_gain,
    q_weight,
    key_matrix,
    value_matrix,
    out_weight,
    label_table,
    refresh_rows,
    label_counts,
    queries,
    positives,
):
    width = hidden_states.shape[1]
    group_tokens = hidden_states.shape[0]
    texts, length = token_ids.shape
    states = hidden_states.astype(jnp.float32)
    scaled = lax.rsqrt(jnp.mean(states * states, axis=1, keepdims=True) + norm_eps)
    normed = (states * scaled * norm_gain).astype(jnp.bfloat16)
    pieces = (
        lax.all_gather(q_weight, "dp", axis=0, tiled=True),
        lax.all_gather(key_matrix, "dp", axis=0, tiled=True),
        lax.all_gather(value_matrix, "dp", axis=0, tiled=True),
    )
    query_raw, key_raw, value_raw = tuple(
        (jnp.dot(normed, piece, preferred_element_type=jnp.float32) for piece in pieces)
    )
    queries_rot = (
        rotary(query_raw.reshape(texts, length, -1, HEAD_WIDTH), HEAD_WIDTH)
        .reshape(group_tokens, -1)
        .astype(jnp.bfloat16)
    )
    rotary_keys = (
        rotary(key_raw.reshape(texts, length, -1, HEAD_WIDTH), HEAD_WIDTH)
        .reshape(group_tokens, -1)
        .astype(jnp.bfloat16)
    )
    values_rot = value_raw.astype(jnp.bfloat16)
    attended = attend(queries_rot, rotary_keys, values_rot, token_ids, HEAD_WIDTH)
    live = (token_ids != 0).astype(jnp.float32)
    share = texts // lax.axis_size("mp")
    member = lax.axis_index("mp")
    live_own = lax.dynamic_slice_in_dim(live, member * share, share, 0)
    states_own = lax.dynamic_slice_in_dim(
        states, member * share * length, share * length, 0
    ).reshape(share, length, width)
    counted = jnp.sum(live_own, axis=1, keepdims=True)
    head_terms = lax.dot_general(
        attended,
        lax.all_gather(out_weight, "dp", axis=0, tiled=True),
        (((1,), (1,)), ((), ())),
        preferred_element_type=jnp.float32,
    )
    output_own = lax.psum_scatter(head_terms, "mp", scatter_dimension=0, tiled=True).reshape(
        share, length, width
    )
    refreshed = (
        jnp.sum((states_own + output_own) * live_own[:, :, None], axis=1) / counted
    ).astype(jnp.bfloat16)
    table = label_table.at[refresh_rows].set(refreshed)
    root = math.sqrt(width)
    owned = label_table.shape[0]
    logits = (
        lax.dot_general(
            queries, table, (((1,), (1,)), ((), ())), preferred_element_type=jnp.float32
        )
        / root
    )
    first_label = (lax.axis_index("dp") * lax.axis_size("mp") + member) * owned
    label_ids = first_label + jnp.arange(owned, dtype=jnp.int32)
    matched = jnp.any(positives[:, :, None] == label_ids[None, None, :], axis=1)
    signs = jnp.where(matched, 1.0, -1.0)
    margin = signs * logits
    balance = (1.0 - focal_beta) / -jnp.expm1(
        label_counts.astype(jnp.float32) * math.log(focal_beta)
    )
    missed = jax.nn.sigmoid(-margin)
    softened = jax.nn.softplus(-margin)
    focal_terms = balance[None, :] * missed * missed * softened
    slopes = (
        balance[None, :]
        * signs
        * (-(missed * missed) * (2.0 * jax.nn.sigmoid(margin) * softened + missed))
    ).astype(jnp.bfloat16)
    query_part = jnp.dot(slopes, table, preferred_element_type=jnp.float32) / root
    label_part = (
        lax.dot_general(
            slopes, queries, (((0,), (0,)), ((), ())), preferred_element_type=jnp.float32
        )
        / root
    )
    query_sum, loss_sum, summed_weight = lax.psum(
        (query_part, jnp.sum(focal_terms), jnp.sum(balance)), ("dp", "mp")
    )
    total_labels = owned * lax.axis_size("dp") * lax.axis_size("mp")
    factor = total_labels / summed_weight
    loss = factor * loss_sum / (queries.shape[0] * total_labels)
    return (factor * label_part, factor * query_sum, loss)


def solution(mesh):
    in_specs = (
        P("dp", None),
        P("dp", None),
        P(),
        P("dp", "mp"),
        P("dp", "mp"),
        P("dp", "mp"),
        P("dp", "mp"),
        P(("dp", "mp"), None),
        P(("dp", "mp")),
        P(("dp", "mp")),
        P(),
        P(),
    )
    out_specs = (P(("dp", "mp"), None), P(), P())
    return jax.shard_map(shards, mesh=mesh, in_specs=in_specs, out_specs=out_specs, check_vma=False)
```

profile of v0, /device:TPU:0, one launch (start us, length us, event | category | flops | bytes accessed | tf_op | source)
XLA Modules:
  0.0 456.2 jit_solution(8268178007199718906)
XLA Ops:
  7.2 0.0 copy-start
  7.2 0.0 copy-start.6
  7.2 0.0 all-gather.3.cloned.1.call-start
  7.2 0.7 all-gather.3.cloned.1.call-update
  7.9 0.0 copy-start.4
  7.9 0.0 all-gather.5.cloned.1.call-start
  8.0 0.7 all-gather.5.cloned.1.call-update
  8.7 0.0 reduce-scatter.2.cloned.1.call-start
  8.7 0.0 copy-done.6
  8.8 0.1 copy.28
  8.9 0.1 fusion.18
  8.9 0.1 pad_maximum_fusion
  9.0 3.0 multiply_reduce_fusion
  12.0 0.0 copy-done.4
  12.0 36.6 %all_gather.13 = bf16[3584,128]{1,0:T(8,128)(2,1)S(1)} all-gather(bf16[448,128]{1,0:T(8,128)(2,1)S(1)} %copy-done.4), channel_id=1, replica_groups=mesh['dp'=8,'mp'=4] {'dp'}, dimensions={0}, use_global_device_ids=true | all-gather | bytes 1032192 | tf_op jit(solution)/shard_map/all_gather | solution.py:67
  48.6 0.0 copy-done.1
  48.6 0.0 copy-done.9
  48.6 1.2 fusion.23
  49.8 0.0 copy-start.5
  49.8 0.1 slice_negate_fusion.1
  49.9 0.1 fusion.10
  50.1 0.1 broadcast_and_fusion
  50.2 0.4 copy-done.5
  50.7 35.5 %all_gather.12 = bf16[3584,128]{1,0:T(8,128)(2,1)S(1)} all-gather(bf16[448,128]{1,0:T(8,128)(2,1)S(1)} %copy-done.5), channel_id=1, replica_groups=mesh['dp'=8,'mp'=4] {'dp'}, dimensions={0}, use_global_device_ids=true | all-gather | bytes 1032192 | tf_op jit(solution)/shard_map/all_gather | solution.py:68
  86.2 1.2 convolution_convert_fusion.1
  87.3 42.0 %all-gather.3.cloned.1.call-done = bf16[3584,896]{1,0:T(8,128)(2,1)} async-done(((bf16[448,896]{1,0:T(8,128)(2,1)}), bf16[3584,896]{1,0:T(8,128)(2,1)}) %all-gather.3.cloned.1.call-update) | async-done | bytes 6422544 | tf_op jit(solution)/shard_map/all_gather | solution.py:66
  129.4 9.2 %fusion.22 = f32[512,896]{1,0:T(8,128)} fusion(bf16[3584,896]{1,0:T(8,128)(2,1)} %all-gather.3.cloned.1.call-done, f32[3584]{0:T(1024)S(1)} %copy-done.9, f32[512]{0:T(512)S(1)} %add_rsqrt_fusion, bf16[512,3584]{1,0:T(8,128)(2,1)} %param.12), kind=kOutput, calls=%fused_computation.58 | convolution fusion | flops 3295674368 | bytes 11943936 | tf_op jit(solution)/shard_map/dot_general | solution.py:71
  138.5 1.8 reshape.123
  140.3 0.8 slice_negate_fusion
  141.1 0.6 maximum_multiply_fusion
  141.7 0.0 copy-start.3
  141.7 0.2 mul.215
  142.0 1.3 copy-done.3
  143.2 1.0 fusion
  144.3 1.0 reshape.124
  145.3 2.0 fusion.25
  147.3 0.5 fusion.1
  147.8 0.3 copy.31
  148.1 84.0 %all-gather.5.cloned.1.call-done = bf16[3584,896]{1,0:T(8,128)(2,1)} async-done(((bf16[448,896]{1,0:T(8,128)(2,1)}), bf16[3584,896]{1,0:T(8,128)(2,1)}) %all-gather.5.cloned.1.call-update) | async-done | bytes 6422544 | tf_op jit(solution)/shard_map/all_gather | solution.py:95
  232.1 8.9 %fusion.4 = f32[512,3584]{1,0:T(8,128)} fusion(bf16[3584,896]{1,0:T(8,128)(2,1)} %all-gather.5.cloned.1.call-done, bf16[64,8,7,128]{3,2,1,0:T(8,128)(2,1)S(1)} %bitcast.69), kind=kOutput, calls=%fused_computation.21 | convolution fusion | flops 3288334336 | bytes 14680064 | tf_op jit(solution)/shard_map/dot_general | solution.py:93
  240.9 0.0 reduce-scatter.2.cloned.1.call-update
  241.0 0.3 all-reduce.3.cloned.1.call-start
  241.2 0.0 copy-start.7
  241.3 0.0 copy-start.10
  241.3 0.0 copy-start.8
  241.3 6.7 %convert_element_type.43 = f32[512,3584]{1,0:T(8,128)} convert(bf16[512,3584]{1,0:T(8,128)(2,1)} %param.12) | non-fusion elementwise | flops 1835008 | bytes 11010048 | tf_op jit(solution)/shard_map/convert_element_type | solution.py:62
  247.9 0.1 dynamic-slice_convert_fusion
  248.0 0.1 copy.32
  248.1 0.1 copy.26
  248.2 0.4 compare_reduce_fusion
  248.6 0.1 copy.27
  248.7 0.1 fusion.19
  248.8 0.6 fusion.24
  249.5 55.3 %reduce-scatter.2.cloned.1.call-done = f32[128,3584]{1,0:T(8,128)} async-done(((f32[512,3584]{1,0:T(8,128)}), f32[128,3584]{1,0:T(8,128)}) %reduce-scatter.2.cloned.1.call-update) | async-done | bytes 1835024 | tf_op jit(solution)/shard_map/reduce_scatter | solution.py:99
  304.8 2.5 multiply_reduce_fusion.1
  307.4 0.0 copy-done.2
  307.4 1.8 scatter_custom_fusion
  309.2 1.3 fusion.14
  310.5 1.8 convolution_multiply_fusion.1
  312.3 0.0 all-reduce.3.cloned.1.call-update
  312.4 39.9 %all-reduce = (f32[]{:T(128)}, f32[]{:T(128)}) all-reduce(f32[]{:T(128)} %get-tuple-element.5, f32[]{:T(128)} %get-tuple-element.15), channel_id=1, replica_groups=mesh['dp'=8,'mp'=4] {'dp','mp'}, use_global_device_ids=true, to_apply=%region_8.9 | all-reduce | flops 2 | bytes 16 | tf_op jit(solution)/shard_map/psum | solution.py:137
  353.6 2.6 convolution_multiply_fusion
  356.2 89.4 %all-reduce.3.cloned.1.call-done = f32[128,3584]{1,0:T(8,128)} async-done(((f32[128,3584]{1,0:T(8,128)}), f32[128,3584]{1,0:T(8,128)}) %all-reduce.3.cloned.1.call-update) | async-done | bytes 1835024 | tf_op jit(solution)/shard_map/psum | solution.py:137
  445.6 2.9 broadcast_multiply_fusion
  (13 shorter events, 0.1 us)
Async XLA Ops:
  7.2 302.1 %copy-start = (bf16[128,3584]{1,0:T(8,128)(2,1)S(1)}, bf16[128,3584]{1,0:T(8,128)(2,1)}, u32[]{:S(2)}) copy-start(bf16[128,3584]{1,0:T(8,128)(2,1)} %param.22) | copy-start | bytes 2752516
  7.2 1.6 copy-start.6
  7.2 122.2 %all-gather.3.cloned.1.call-start = ((), (), s32[]{:S(2)}) async-start(), calls=%async_computation.1 | async-start | bytes 7225344 | tf_op jit(solution)/shard_map/all_gather | solution.py:66
  7.9 4.1 copy-start.4
  7.9 224.2 %all-gather.5.cloned.1.call-start = ((), (), s32[]{:S(2)}) async-start(), calls=%async_computation.2 | async-start | bytes 7225344 | tf_op jit(solution)/shard_map/all_gather | solution.py:95
  8.7 296.1 %reduce-scatter.2.cloned.1.call-start = ((), (), s32[]{:S(2)}) async-start(), calls=%async_computation.3 | async-start | bytes 9175040 | tf_op jit(solution)/shard_map/reduce_scatter | solution.py:99
  9.0 39.6 %copy-start.1 = (bf16[512,3584]{1,0:T(8,128)(2,1)S(1)}, bf16[512,3584]{1,0:T(8,128)(2,1)}, u32[]{:S(2)}) copy-start(bf16[512,3584]{1,0:T(8,128)(2,1)} %param.12) | copy-start | bytes 11010052
  9.0 39.6 %copy-start.9 = (f32[3584]{0:T(1024)S(1)}, f32[3584]{0:T(1024)}, u32[]{:S(2)}) copy-start(f32[3584]{0:T(1024)} %param.14) | copy-start | bytes 43012
  49.8 0.9 copy-start.5
  141.7 1.5 copy-start.3
  241.0 204.6 %all-reduce.3.cloned.1.call-start = ((), (), s32[]{:S(2)}) async-start(), calls=%async_computation.4 | async-start | bytes 3670016 | tf_op jit(solution)/shard_map/psum | solution.py:137
  241.2 6.8 %copy-start.7 = (s32[128,8]{0,1:T(8,128)S(1)}, s32[128,8]{0,1:T(8,128)}, u32[]{:S(2)}) copy-start(s32[128,8]{0,1:T(8,128)} %param.23) | copy-start | bytes 12292
  241.3 7.6 %copy-start.10 = (s32[8]{0:T(128)S(1)}, s32[8]{0:T(128)}, u32[]{:S(2)}) copy-start(s32[8]{0:T(128)} %param.20) | copy-start | bytes 100
  241.3 7.6 %copy-start.8 = (s32[256]{0:T(256)S(1)}, s32[256]{0:T(256)}, u32[]{:S(2)}) copy-start(s32[256]{0:T(256)} %param.21) | copy-start | bytes 3076
  247.9 59.4 %copy-start.2 = (bf16[256,3584]{1,0:T(8,128)(2,1)S(1)}, bf16[256,3584]{1,0:T(8,128)(2,1)}, u32[]{:S(2)}) copy-start(bf16[256,3584]{1,0:T(8,128)(2,1)} %param.19) | copy-start | bytes 5505028
Sparse Core Ops, SparseCore 0:
  10.2 119.1 all-gather.2
  131.5 100.5 all-gather.4
  241.1 63.6 reduce-scatter.1
  312.5 133.0 all-reduce.2
where the time goes:
time: 457 us; the launch traced here: 456 us
  waiting for transfers between devices  272 us (60%)
  blocking collectives  112 us (25%)
  matrix products  28.6 us (6%)
  other arithmetic  21.1 us (5%)
  between operations  16.5 us (4%)
  local copies, waits for them, and re-layouts  5.46 us (1%)
    psum x1, waiting for transfers between devices, shards(): lax.psum((query_part, jnp.sum(focal_terms), jnp.sum(balance)), ('dp', 'mp'))  89.4 us
    all_gather x1, waiting for transfers between devices, shards(): lax.all_gather(out_weight, 'dp', axis=0, tiled=True)  84 us
    reduce_scatter x1, waiting for transfers between devices, shards(): lax.psum_scatter(head_terms, 'mp', scatter_dimension=0, tiled=True)  55.3 us
    all_gather x1, waiting for transfers between devices, shards(): lax.all_gather(q_weight, 'dp', axis=0, tiled=True)  42 us
    psum x1, blocking collectives, shards(): lax.psum((query_part, jnp.sum(focal_terms), jnp.sum(balance)), ('dp', 'mp'))  39.9 us
    all_gather x1, blocking collectives, shards(): lax.all_gather(key_matrix, 'dp', axis=0, tiled=True)  36.6 us
    all_gather x1, blocking collectives, shards(): lax.all_gather(value_matrix, 'dp', axis=0, tiled=True)  35.5 us
    dot_general x3, matrix products, shards(): jnp.dot(normed, piece, preferred_element_type=jnp.float32)  11.5 us
  transfers between devices with their start and end apart: 4, of which 4 were waited for; matrix products, arithmetic and copies ran while one was open for 7% of the time, Pallas kernels for 0%

commit v1 on v0

--- a/solution.py
+++ b/solution.py
@@ -62,14 +62,15 @@
     states = hidden_states.astype(jnp.float32)
     scaled = lax.rsqrt(jnp.mean(states * states, axis=1, keepdims=True) + norm_eps)
     normed = (states * scaled * norm_gain).astype(jnp.bfloat16)
-    pieces = (
-        lax.all_gather(q_weight, "dp", axis=0, tiled=True),
-        lax.all_gather(key_matrix, "dp", axis=0, tiled=True),
-        lax.all_gather(value_matrix, "dp", axis=0, tiled=True),
+    heads = q_weight.shape[1]
+    kv = key_matrix.shape[1]
+    weights = lax.all_gather(
+        jnp.concatenate([q_weight, key_matrix, value_matrix], axis=1), "dp", axis=0, tiled=True
     )
-    query_raw, key_raw, value_raw = tuple(
-        (jnp.dot(normed, piece, preferred_element_type=jnp.float32) for piece in pieces)
-    )
+    raw = jnp.dot(normed, weights, preferred_element_type=jnp.float32)
+    query_raw = raw[:, :heads]
+    key_raw = raw[:, heads : heads + kv]
+    value_raw = raw[:, heads + kv :]
     queries_rot = (
         rotary(query_raw.reshape(texts, length, -1, HEAD_WIDTH), HEAD_WIDTH)
         .reshape(group_tokens, -1)
@@ -83,64 +84,93 @@
     values_rot = value_raw.astype(jnp.bfloat16)
     attended = attend(queries_rot, rotary_keys, values_rot, token_ids, HEAD_WIDTH)
     live = (token_ids != 0).astype(jnp.float32)
-    share = texts // lax.axis_size("mp")
+    counted = jnp.sum(live, axis=1, keepdims=True)
+    pooled = (
+        jnp.sum(attended.astype(jnp.float32).reshape(texts, length, -1) * live[:, :, None], axis=1)
+        / counted
+    ).astype(jnp.bfloat16)
+    groups = lax.axis_size("dp")
+    members = lax.axis_size("mp")
+    share = texts // members
     member = lax.axis_index("mp")
     live_own = lax.dynamic_slice_in_dim(live, member * share, share, 0)
     states_own = lax.dynamic_slice_in_dim(
-        states, member * share * length, share * length, 0
+        hidden_states, member * share * length, share * length, 0
     ).reshape(share, length, width)
-    counted = jnp.sum(live_own, axis=1, keepdims=True)
-    head_terms = lax.dot_general(
-        attended,
-        lax.all_gather(out_weight, "dp", axis=0, tiled=True),
-        (((1,), (1,)), ((), ())),
-        preferred_element_type=jnp.float32,
+    counted_own = jnp.sum(live_own, axis=1, keepdims=True)
+    base_own = (
+        jnp.sum(states_own.astype(jnp.float32) * live_own[:, :, None], axis=1) / counted_own
     )
-    output_own = lax.psum_scatter(head_terms, "mp", scatter_dimension=0, tiled=True).reshape(
-        share, length, width
-    )
-    refreshed = (
-        jnp.sum((states_own + output_own) * live_own[:, :, None], axis=1) / counted
-    ).astype(jnp.bfloat16)
-    table = label_table.at[refresh_rows].set(refreshed)
+    pooled_all = lax.all_gather(pooled, "dp", axis=0, tiled=True)
+    terms = lax.dot_general(
+        pooled_all, out_weight, (((1,), (1,)), ((), ())), preferred_element_type=jnp.float32
+    ).reshape(groups, members, share, -1)
+    mine = lax.psum_scatter(terms, "mp", scatter_dimension=1, tiled=True)
+    mine = mine.reshape(groups, share, -1)
+    swapped = lax.all_to_all(mine, "dp", 0, 0, tiled=True)
+    projected = jnp.swapaxes(swapped, 0, 1).reshape(share, width)
+    refreshed = (base_own + projected).astype(jnp.bfloat16)
+
     root = math.sqrt(width)
     owned = label_table.shape[0]
+    first_label = (lax.axis_index("dp") * members + member) * owned
+    label_ids = first_label + jnp.arange(owned, dtype=jnp.int32)
+    balance = balances(label_counts)
+    replaced = jnp.any(
+        refresh_rows[:, None] == jnp.arange(owned, dtype=jnp.int32)[None, :], axis=0
+    )
+    kept = jnp.where(replaced, 0.0, balance)
+    early_slopes, early_loss = focal(queries, label_table, positives, label_ids, kept, root)
+    query_part = jnp.dot(early_slopes, label_table, preferred_element_type=jnp.float32) / root
+    query_sum, loss_sum, summed_weight = lax.psum(
+        (query_part, early_loss, jnp.sum(balance)), ("dp", "mp")
+    )
+    new_ids = lax.all_gather(first_label + refresh_rows, ("dp", "mp"), axis=0, tiled=True)
+    new_balance = lax.all_gather(balance[refresh_rows], ("dp", "mp"), axis=0, tiled=True)
+    refreshed_all = lax.all_gather(refreshed, ("dp", "mp"), axis=0, tiled=True)
+    late_slopes, late_loss = focal(queries, refreshed_all, positives, new_ids, new_balance, root)
+    query_late = jnp.dot(late_slopes, refreshed_all, preferred_element_type=jnp.float32) / root
+    own_late = lax.dynamic_slice_in_dim(
+        late_slopes, (lax.axis_index("dp") * members + member) * share, share, 1
+    )
+    slopes = early_slopes.at[:, refresh_rows].set(own_late)
+    label_part = (
+        lax.dot_general(
+            slopes, queries, (((0,), (0,)), ((), ())), preferred_element_type=jnp.float32
+        )
+        / root
+    )
+    total_labels = owned * groups * members
+    factor = total_labels / summed_weight
+    loss = factor * (loss_sum + late_loss) / (queries.shape[0] * total_labels)
+    return (factor * label_part, factor * (query_sum + query_late), loss)
+
+
+def balances(label_counts):
+    return (1.0 - focal_beta) / -jnp.expm1(
+        label_counts.astype(jnp.float32) * math.log(focal_beta)
+    )
+
+
+def focal(queries, table, positives, label_ids, balance, root):
     logits = (
         lax.dot_general(
             queries, table, (((1,), (1,)), ((), ())), preferred_element_type=jnp.float32
         )
         / root
     )
-    first_label = (lax.axis_index("dp") * lax.axis_size("mp") + member) * owned
-    label_ids = first_label + jnp.arange(owned, dtype=jnp.int32)
     matched = jnp.any(positives[:, :, None] == label_ids[None, None, :], axis=1)
     signs = jnp.where(matched, 1.0, -1.0)
     margin = signs * logits
-    balance = (1.0 - focal_beta) / -jnp.expm1(
-        label_counts.astype(jnp.float32) * math.log(focal_beta)
-    )
     missed = jax.nn.sigmoid(-margin)
     softened = jax.nn.softplus(-margin)
-    focal_terms = balance[None, :] * missed * missed * softened
+    loss = jnp.sum(balance[None, :] * missed * missed * softened)
     slopes = (
         balance[None, :]
         * signs
         * (-(missed * missed) * (2.0 * jax.nn.sigmoid(margin) * softened + missed))
     ).astype(jnp.bfloat16)
-    query_part = jnp.dot(slopes, table, preferred_element_type=jnp.float32) / root
-    label_part = (
-        lax.dot_general(
-            slopes, queries, (((0,), (0,)), ((), ())), preferred_element_type=jnp.float32
-        )
-        / root
-    )
-    query_sum, loss_sum, summed_weight = lax.psum(
-        (query_part, jnp.sum(focal_terms), jnp.sum(balance)), ("dp", "mp")
-    )
-    total_labels = owned * lax.axis_size("dp") * lax.axis_size("mp")
-    factor = total_labels / summed_weight
-    loss = factor * loss_sum / (queries.shape[0] * total_labels)
-    return (factor * label_part, factor * query_sum, loss)
+    return slopes, loss
 
 
 def solution(mesh):

time: 457 us -> 445 us (0.974)
  waiting for transfers between devices: 272 us -> 258 us
  local copies, waits for them, and re-layouts: 5.46 us -> 13 us
  other arithmetic: 21.1 us -> 15.6 us
  starting transfers between devices: 0.38 us -> 5.86 us
    unnamed x0 -> x2, blocking collectives: none -> 78.6 us
    reduce_scatter x1 -> x0, waiting for transfers between devices: 55.3 us -> none  [shards(): lax.psum_scatter(head_terms, 'mp', scatter_dimension=0, tiled=True)]
    all_gather x2 -> x1, blocking collectives: 72.1 us -> 31.3 us  [shards(): pooled_all = lax.all_gather(pooled, 'dp', axis=0, tiled=True)]
    psum x1 -> x0, blocking collectives: 39.9 us -> none  [shards(): lax.psum((query_part, jnp.sum(focal_terms), jnp.sum(balance)), ('dp', 'mp'))]
    unnamed x4 -> x5, waiting for transfers between devices: 1.41 us -> 31 us
    psum x1, waiting for transfers between devices: 89.4 us -> 97.6 us  [shards(): lax.psum((query_part, early_loss, jnp.sum(balance)), ('dp', 'mp'))]
    convert_element_type x1 -> x2, other arithmetic: 6.66 us -> 0.79 us  [the longest x1 0.71 us: shards(): refreshed = (base_own + projected).astype(jnp.bfloat16)]
    all_to_all x0 -> x1, starting transfers between devices: none -> 5.52 us  [shards(): swapped = lax.all_to_all(mine, 'dp', 0, 0, tiled=True)]
  transfers between devices with their start and end apart: 4 -> 5, of which waited for: 4 -> 4; matrix products, arithmetic and copies ran while one was open for 7% -> 4% of each run, Pallas kernels for 0% -> 0%
where the time goes in v1:
time: 445 us
  waiting for transfers between devices  258 us (58%)
  blocking collectives  110 us (25%)
  matrix products  25.7 us (6%)
  between operations  17.2 us (4%)
  other arithmetic  15.6 us (4%)
  local copies, waits for them, and re-layouts  13 us (3%)
  starting transfers between devices  5.86 us (1%)
    all_gather x1, waiting for transfers between devices, shards(): lax.all_gather(jnp.concatenate([q_weight, key_matrix, value_matrix], axis...  124 us
    psum x1, waiting for transfers between devices, shards(): lax.psum((query_part, early_loss, jnp.sum(balance)), ('dp', 'mp'))  97.6 us
    unnamed x2, blocking collectives  78.6 us
    all_gather x1, blocking collectives, shards(): pooled_all = lax.all_gather(pooled, 'dp', axis=0, tiled=True)  31.3 us
    unnamed x5, waiting for transfers between devices  31 us
    dot_general x1, matrix products, shards(): raw = jnp.dot(normed, weights, preferred_element_type=jnp.float32)  9.42 us
  transfers between devices with their start and end apart: 5, of which 4 were waited for; matrix products, arithmetic and copies ran while one was open for 4% of the time, Pallas kernels for 0%

profile of v1, /device:TPU:0, one launch (start us, length us, event | category | flops | bytes accessed | tf_op | source)
XLA Modules:
  0.0 444.8 jit_solution(116062743867382370)
XLA Ops:
  7.2 0.0 all-gather.4.cloned.1.call-start
  7.2 2.4 pad_maximum_fusion
  9.7 0.0 all-gather.4.cloned.1.call-update
  9.7 0.0 all-reduce.9.cloned.1.call-start
  9.8 0.1 copy.48
  9.9 0.1 copy.51
  10.0 0.1 fusion.32
  10.0 0.1 pad_maximum_fusion.1
  10.1 2.8 fusion
  13.0 0.1 broadcast_and_fusion
  13.1 123.6 %all-gather.4.cloned.1.call-done = bf16[3584,1152]{1,0:T(8,128)(2,1)} async-done(((bf16[448,1152]{1,0:T(8,128)(2,1)}), bf16[3584,1152]{1,0:T(8,128)(2,1)}) %all-gather.4.cloned.1.call-update) | async-done | bytes 8257552 | tf_op jit(solution)/shard_map/all_gather | solution.py:67
  136.7 9.4 %fusion.5 = f32[512,1152]{1,0:T(8,128)S(1)} fusion(bf16[3584,1152]{1,0:T(8,128)(2,1)} %all-gather.4.cloned.1.call-done, bf16[512,3584]{1,0:T(8,128)(2,1)} %param.12, f32[3584]{0:T(1024)S(1)} %copy-done.10, f32[512]{0:T(512)S(1)} %add_rsqrt_fusion), kind=kOutput, calls=%fused_computation.12 | convolution fusion | flops 4235198464 | bytes 14303232 | tf_op jit(solution)/shard_map/dot_general | solution.py:70
  146.2 1.4 slice.35
  147.6 0.6 copy-done.1
  148.2 2.7 reshape.141
  150.9 3.1 slice_negate_fusion
  154.0 0.6 maximum_multiply_fusion
  154.6 0.2 mul.275
  154.8 0.8 copy-done.2
  155.7 1.0 fusion.9
  156.7 2.0 reshape.142
  158.7 0.1 slice_negate_fusion.1
  158.8 1.2 fusion.21
  160.0 2.0 fusion.36
  162.1 0.7 fusion.10
  162.8 0.1 fusion.30
  162.9 31.3 %all_gather.18 = bf16[256,896]{1,0:T(8,128)(2,1)S(1)} all-gather(bf16[32,896]{1,0:T(8,128)(2,1)S(1)} %fusion.30), channel_id=1, replica_groups=mesh['dp'=8,'mp'=4] {'dp'}, dimensions={0}, use_global_device_ids=true | all-gather | bytes 516096 | tf_op jit(solution)/shard_map/all_gather | solution.py:104
  194.2 1.3 fusion.37
  195.4 0.0 all-reduce.9.cloned.1.call-update
  195.5 0.6 dynamic-slice
  196.1 30.9 %all-reduce.9.cloned.1.call-done = f32[8,4,8,448]{3,2,1,0:T(8,128)} async-done(((f32[8,4,8,448]{3,2,1,0:T(8,128)}), f32[8,4,8,448]{3,2,1,0:T(8,128)}) %all-reduce.9.cloned.1.call-update) | async-done | bytes 458768
  227.0 2.2 dynamic-slice_bitcast_fusion
  229.2 5.5 %all-to-all-start = ((f32[8,8,448]{2,1,0:T(8,128)}), f32[8,8,448]{2,1,0:T(8,128)S(1)}, u32[]{:S(2)}, u32[]{:S(2)}) async-start(f32[8,8,448]{2,1,0:T(8,128)} %dynamic-slice_bitcast_fusion), calls=%async_computation | async-start | bytes 262144 | tf_op jit(solution)/shard_map/all_to_all | solution.py:110
  234.7 0.2 all-gather.6.cloned.1.call-start
  234.9 0.1 fusion.35
  235.0 0.1 copy.47
  235.1 1.6 fusion.11
  236.7 5.3 %all-to-all-done = f32[8,8,448]{2,1,0:T(8,128)S(1)} async-done(((f32[8,8,448]{2,1,0:T(8,128)}), f32[8,8,448]{2,1,0:T(8,128)S(1)}, u32[]{:S(2)}, u32[]{:S(2)}) %all-to-all-start) | async-done | bytes 114720 | tf_op jit(solution)/shard_map/all_to_all | solution.py:110
  242.1 0.1 copy.53
  242.1 0.1 reshape.146
  242.2 0.7 add_convert_fusion
  243.0 0.0 all-gather.6.cloned.1.call-update
  243.0 0.0 all-reduce.7.cloned.1.call-start
  243.0 0.1 copy.46
  243.2 0.1 compare_select_fusion.2
  243.3 37.7 %all-reduce.1 = s32[256]{0:T(256)S(1)} all-reduce(s32[256]{0:T(256)S(1)} %get-tuple-element.25), channel_id=1, replica_groups=mesh['dp'=8,'mp'=4] {'dp','mp'}, use_global_device_ids=true, to_apply=%add.1 | all-reduce | flops 256 | bytes 2048
  281.0 0.1 fusion.33
  281.1 0.7 compare_reduce_fusion
  281.8 0.6 fusion.34
  282.4 1.5 fusion.27
  283.9 1.7 convolution_multiply_fusion.2
  285.6 0.0 all-reduce.7.cloned.1.call-update
  285.6 0.1 copy.55
  285.7 0.6 gather_fusion
  286.4 0.2 dynamic-update-slice
  286.6 40.9 %all-reduce.3 = (f32[256]{0:T(256)S(1)}, f32[]{:T(128)}, f32[]{:T(128)}) all-reduce(f32[256]{0:T(256)S(1)} %dynamic-update-slice, f32[]{:T(128)} %get-tuple-element.8, f32[]{:T(128)} %get-tuple-element.20), channel_id=2, replica_groups=mesh['dp'=8,'mp'=4] {'dp','mp'}, use_global_device_ids=true, to_apply=%add | all-reduce | flops 258 | bytes 2064
  328.2 0.0 all-gather.6.cloned.1.call-done
  328.2 3.0 fusion.29
  331.2 0.1 dynamic-slice_bitcast_fusion.1
  331.3 0.1 copy.56
  332.7 0.7 scatter_fusion
  333.4 2.5 convolution_multiply_fusion
  335.8 97.6 %all-reduce.7.cloned.1.call-done = f32[128,3584]{1,0:T(8,128)} async-done(((f32[128,3584]{1,0:T(8,128)}), f32[128,3584]{1,0:T(8,128)}) %all-reduce.7.cloned.1.call-update) | async-done | bytes 1835024 | tf_op jit(solution)/shard_map/psum | solution.py:125
  433.4 3.7 fusion.4
  (35 shorter events, 0.1 us)
Async XLA Ops:
  7.2 275.3 %copy-start = (bf16[256,3584]{1,0:T(8,128)(2,1)S(1)}, bf16[256,3584]{1,0:T(8,128)(2,1)}, u32[]{:S(2)}) copy-start(bf16[256,3584]{1,0:T(8,128)(2,1)} %param.19) | copy-start | bytes 5505028
  7.2 2.6 copy-start.6
  7.2 129.5 %all-gather.4.cloned.1.call-start = ((), (), s32[]{:S(2)}) async-start(), calls=%async_computation.1 | async-start | bytes 9289728 | tf_op jit(solution)/shard_map/all_gather | solution.py:67
  9.7 217.3 %all-reduce.9.cloned.1.call-start = ((), (), s32[]{:S(2)}) async-start(), calls=%async_computation.4 | async-start | bytes 1048576
  10.1 126.6 %copy-start.10 = (f32[3584]{0:T(1024)S(1)}, f32[3584]{0:T(1024)}, u32[]{:S(2)}) copy-start(f32[3584]{0:T(1024)} %param.14) | copy-start | bytes 43012
  146.2 2.0 copy-start.1
  154.0 1.7 copy-start.2
  156.7 2.0 slice-start
  158.7 1.3 copy-start.3
  162.1 32.1 %copy-start.5 = (bf16[448,896]{1,0:T(8,128)(2,1)S(1)}, bf16[448,896]{1,0:T(8,128)(2,1)}, u32[]{:S(2)}) copy-start(bf16[448,896]{1,0:T(8,128)(2,1)} %param.18) | copy-start | bytes 2408452
  162.8 32.7 %copy-start.11 = (u32[32]{0:T(128)S(1)}, u32[32]{0:T(128)}, u32[]{:S(2)}) copy-start(u32[32]{0:T(128)} %constant.85) | copy-start | bytes 388
  195.4 47.6 %copy-start.7 = (s32[128,8]{0,1:T(8,128)S(1)}, s32[128,8]{0,1:T(8,128)}, u32[]{:S(2)}) copy-start(s32[128,8]{0,1:T(8,128)} %param.23) | copy-start | bytes 12292
  195.4 47.7 %copy-start.9 = (s32[8]{0:T(128)S(1)}, s32[8]{0:T(128)}, u32[]{:S(2)}) copy-start(s32[8]{0:T(128)} %param.20) | copy-start | bytes 100
  195.4 86.4 %copy-start.8 = (s32[256]{0:T(256)S(1)}, s32[256]{0:T(256)}, u32[]{:S(2)}) copy-start(s32[256]{0:T(256)} %param.21) | copy-start | bytes 3076
  195.4 87.0 %copy-start.4 = (bf16[128,3584]{1,0:T(8,128)(2,1)S(1)}, bf16[128,3584]{1,0:T(8,128)(2,1)}, u32[]{:S(2)}) copy-start(bf16[128,3584]{1,0:T(8,128)(2,1)} %param.22) | copy-start | bytes 2752516
  229.2 12.9 %all-to-all-start = ((f32[8,8,448]{2,1,0:T(8,128)}), f32[8,8,448]{2,1,0:T(8,128)S(1)}, u32[]{:S(2)}, u32[]{:S(2)}) async-start(f32[8,8,448]{2,1,0:T(8,128)} %dynamic-slice_bitcast_fusion), calls=%async_computation | async-start | bytes 262144 | tf_op jit(solution)/shard_map/all_to_all | solution.py:110
  234.7 93.5 %all-gather.6.cloned.1.call-start = ((), (), s32[]{:S(2)}) async-start(), calls=%async_computation.2 | async-start | bytes 1892352 | tf_op jit(solution)/shard_map/all_gather | solution.py:130
  243.0 190.4 %all-reduce.7.cloned.1.call-start = ((), (), s32[]{:S(2)}) async-start(), calls=%async_computation.3 | async-start | bytes 3670016 | tf_op jit(solution)/shard_map/psum | solution.py:125
Sparse Core Ops, SparseCore 0:
  10.8 125.8 all-gather.3
  195.6 31.3 all-reduce.8
  243.1 52.6 all-gather.5
  301.6 131.7 all-reduce.6

commit v2 on v1

--- a/solution.py
+++ b/solution.py
@@ -1,9 +1,14 @@
+import functools
 import math
 
 import jax
 import jax.numpy as jnp
 from jax import lax
+from jax.experimental import pallas as pl
+from jax.experimental.pallas import tpu as pltpu
 from jax.sharding import PartitionSpec as P
+
+MESH = pl.DeviceIdType.MESH
 
 HEAD_WIDTH = 128
 
@@ -40,6 +45,290 @@
     probs = (weights / jnp.sum(weights, axis=-1, keepdims=True)).astype(jnp.bfloat16)
     mixed = jnp.einsum("ngrts,nsgd->ntgrd", probs, value_r, preferred_element_type=jnp.float32)
     return mixed.reshape(texts * length, -1).astype(jnp.bfloat16)
+
+
+def remote(source, target, send, receive, device):
+    return pltpu.make_async_remote_copy(
+        src_ref=source,
+        dst_ref=target,
+        send_sem=send,
+        recv_sem=receive,
+        device_id=device,
+        device_id_type=MESH,
+    )
+
+
+def each(low, high, body):
+    def run(index, carry):
+        body(index)
+        return carry
+
+    lax.fori_loop(low, high, run, 0)
+
+
+def spread(groups, members, blocks, group_sem, far_sem, core_sem, relay_sem, arrived):
+    group, member = lax.axis_index("dp"), lax.axis_index("mp")
+    far = lax.rem(member + 2, members)
+    core = member + 1 - 2 * lax.rem(member, 2)
+    far_core = lax.rem(core + 2, members)
+
+    def copy(at, slot, sems, index, device):
+        return remote(blocks.at[slot], blocks.at[slot], sems.at[index], arrived.at[slot], device)
+
+    def forward(at):
+        slot = at * members + member
+        copy(at, slot, far_sem, at, (group, far)).start()
+        copy(at, slot, core_sem, at, (group, core)).start()
+
+    def send(step):
+        slot = group * members + member
+        copy(group, slot, group_sem, step, (lax.rem(group + step, groups), member)).start()
+
+    def pass_on(step):
+        at = lax.rem(group + groups - step, groups)
+        slot = at * members + member
+        copy(at, slot, group_sem, step, (at, member)).wait_recv()
+        forward(at)
+
+    def relay(step):
+        at = lax.rem(group + groups - step, groups)
+        slot = at * members + far
+        copy(at, slot, far_sem, at, (group, far)).wait_recv()
+        copy(at, slot, relay_sem, at, (group, core)).start()
+
+    def finish(at):
+        copy(at, at * members + core, core_sem, at, (group, core)).wait_recv()
+        copy(at, at * members + far_core, relay_sem, at, (group, core)).wait_recv()
+        copy(at, at * members + member, far_sem, at, (group, far)).wait_send()
+        copy(at, at * members + member, core_sem, at, (group, core)).wait_send()
+        copy(at, at * members + far, relay_sem, at, (group, core)).wait_send()
+
+    def sent(step):
+        slot = group * members + member
+        copy(group, slot, group_sem, step, (lax.rem(group + step, groups), member)).wait_send()
+
+    each(1, groups, send)
+    forward(group)
+    each(1, groups, pass_on)
+    each(0, groups, relay)
+    each(0, groups, finish)
+    each(1, groups, sent)
+
+
+def spread_sems(groups, members):
+    return [
+        pltpu.SemaphoreType.DMA((groups,)),
+        pltpu.SemaphoreType.DMA((groups,)),
+        pltpu.SemaphoreType.DMA((groups,)),
+        pltpu.SemaphoreType.DMA((groups,)),
+        pltpu.SemaphoreType.DMA((groups * members,)),
+    ]
+
+
+def early_kernel(
+    groups, members, part, meta, blocks, got, sums, terms, s1, r1, s2, r2, *sems
+):
+    group, member = lax.axis_index("dp"), lax.axis_index("mp")
+    own = group * members + member
+    rows = part.shape[1] // members
+    barrier = pltpu.get_barrier_semaphore()
+
+    def greet_member(step):
+        peer = lax.rem(member + step, members)
+        pl.semaphore_signal(barrier, inc=1, device_id=(group, peer), device_id_type=MESH)
+
+    def greet_group(step):
+        peer = lax.rem(group + step, groups)
+        pl.semaphore_signal(barrier, inc=1, device_id=(peer, member), device_id_type=MESH)
+
+    each(1, members, greet_member)
+    each(1, groups, greet_group)
+    pl.semaphore_wait(barrier, groups + members - 2)
+
+    def member_copy(step):
+        peer = lax.rem(member + step, members)
+        start = pl.multiple_of(peer * rows, rows)
+        return remote(
+            part.at[:, pl.ds(start, rows), :],
+            got.at[member],
+            s1.at[step],
+            r1.at[member],
+            (group, peer),
+        )
+
+    def member_wait(step):
+        source = lax.rem(member + members - step, members)
+        remote(
+            got.at[source], got.at[source], s1.at[step], r1.at[source], (group, source)
+        ).wait_recv()
+
+    each(1, members, lambda step: member_copy(step).start())
+    each(1, members, member_wait)
+    first = pl.multiple_of(member * rows, rows)
+
+    def add_members(at):
+        total = part[at, pl.ds(first, rows), :]
+        for step in range(1, members):
+            total = total + got[lax.rem(member + step, members), at]
+        sums[at] = total
+
+    each(0, groups, add_members)
+
+    def group_copy(step):
+        peer = lax.rem(group + step, groups)
+        return remote(sums.at[peer], terms.at[group], s2.at[step], r2.at[group], (peer, member))
+
+    def group_wait(step):
+        source = lax.rem(group + groups - step, groups)
+        remote(
+            terms.at[source], terms.at[source], s2.at[step], r2.at[source], (source, member)
+        ).wait_recv()
+
+    each(1, groups, lambda step: group_copy(step).start())
+    each(1, groups, group_wait)
+    total = sums[group]
+    for step in range(1, groups):
+        total = total + terms[lax.rem(group + step, groups)]
+    blocks[own, :rows] = total
+    blocks[own, rows:] = meta[...]
+    spread(groups, members, blocks, *sems)
+    each(1, members, lambda step: member_copy(step).wait_send())
+    each(1, groups, lambda step: group_copy(step).wait_send())
+
+
+def early_reduce(part, meta, groups, members):
+    _, batch, block = part.shape
+    rows = batch // members
+    return pl.pallas_call(
+        functools.partial(early_kernel, groups, members),
+        out_shape=jax.ShapeDtypeStruct(
+            (groups * members, rows + meta.shape[0], block), jnp.float32
+        ),
+        in_specs=[pl.BlockSpec(memory_space=pltpu.VMEM)] * 2,
+        out_specs=pl.BlockSpec(memory_space=pltpu.VMEM),
+        scratch_shapes=[
+            pltpu.VMEM((members, groups, rows, block), jnp.float32),
+            pltpu.VMEM((groups, rows, block), jnp.float32),
+            pltpu.VMEM((groups, rows, block), jnp.float32),
+            pltpu.SemaphoreType.DMA((members,)),
+            pltpu.SemaphoreType.DMA((members,)),
+            pltpu.SemaphoreType.DMA((groups,)),
+            pltpu.SemaphoreType.DMA((groups,)),
+            *spread_sems(groups, members),
+        ],
+        compiler_params=pltpu.CompilerParams(
+            collective_id=0, has_side_effects=True, vmem_limit_bytes=24 << 20
+        ),
+        name="early_reduce",
+    )(part, meta)
+
+
+def tail_kernel(
+    groups, members, pooled, weight, base, blocks, pool, terms, parts, s1, r1, s2, r2, *sems
+):
+    group, member = lax.axis_index("dp"), lax.axis_index("mp")
+    own = group * members + member
+    devices = groups * members
+    share = terms.shape[1]
+    barrier = pltpu.get_barrier_semaphore()
+
+    def greet(step):
+        peer = lax.rem(own + step, devices)
+        pl.semaphore_signal(
+            barrier,
+            inc=1,
+            device_id=(peer // members, lax.rem(peer, members)),
+            device_id_type=MESH,
+        )
+
+    each(1, devices, greet)
+    pl.semaphore_wait(barrier, devices - 1)
+
+    def pool_copy(step):
+        peer = lax.rem(group + step, groups)
+        return remote(pooled, pool.at[group], s1.at[step], r1.at[group], (peer, member))
+
+    def part_copy(owner_group, owner_member):
+        slot = owner_group * members + owner_member
+        return remote(
+            terms.at[slot], parts.at[own], s2.at[slot], r2.at[own], (owner_group, owner_member)
+        )
+
+    def product(at, rows):
+        made = jnp.dot(rows, weight[...], preferred_element_type=jnp.float32)
+        for index in range(members):
+            terms[at * members + index] = made[index * share : (index + 1) * share]
+
+    def project(step):
+        at = lax.rem(group + groups - step, groups)
+        remote(pooled, pool.at[at], s1.at[step], r1.at[at], (at, member)).wait_recv()
+        product(at, pool[at])
+        each(0, members, lambda index: part_copy(at, index).start())
+
+    each(1, groups, lambda step: pool_copy(step).start())
+    product(group, pooled[...])
+    each(1, members, lambda step: part_copy(group, lax.rem(member + step, members)).start())
+    parts[own] = terms[own]
+    each(1, groups, project)
+
+    def part_wait(step):
+        source = lax.rem(own + devices - step, devices)
+        remote(
+            terms.at[source],
+            parts.at[source],
+            s2.at[source],
+            r2.at[source],
+            (source // members, lax.rem(source, members)),
+        ).wait_recv()
+
+    each(1, devices, part_wait)
+    rows = []
+    for at in range(groups):
+        total = base[at]
+        for index in range(members):
+            total = total + parts[at * members + index]
+        rows.append(total)
+    blocks[own] = jnp.concatenate(rows, axis=0).astype(jnp.bfloat16)
+    spread(groups, members, blocks, *sems)
+    each(1, groups, lambda step: pool_copy(step).wait_send())
+
+    def part_sent(step):
+        slot = lax.rem(own + step, devices)
+        part_copy(slot // members, lax.rem(slot, members)).wait_send()
+
+    each(1, devices, part_sent)
+
+
+def tail(pooled, weight, base, groups, members):
+    texts, heads = pooled.shape
+    block = weight.shape[1]
+    share = texts // members
+    devices = groups * members
+    return pl.pallas_call(
+        functools.partial(tail_kernel, groups, members),
+        out_shape=jax.ShapeDtypeStruct((devices, groups * share, block), jnp.bfloat16),
+        in_specs=[pl.BlockSpec(memory_space=pltpu.VMEM)] * 3,
+        out_specs=pl.BlockSpec(memory_space=pltpu.VMEM),
+        scratch_shapes=[
+            pltpu.VMEM((groups, texts, heads), jnp.bfloat16),
+            pltpu.VMEM((devices, share, block), jnp.float32),
+            pltpu.VMEM((devices, share, block), jnp.float32),
+            pltpu.SemaphoreType.DMA((groups,)),
+            pltpu.SemaphoreType.DMA((groups,)),
+            pltpu.SemaphoreType.DMA((devices,)),
+            pltpu.SemaphoreType.DMA((devices,)),
+            *spread_sems(groups, members),
+        ],
+        compiler_params=pltpu.CompilerParams(
+            collective_id=1, has_side_effects=True, vmem_limit_bytes=24 << 20
+        ),
+        name="tail",
+    )(pooled, weight, base)
+
+
+def kernels_fit(groups, members, width, share):
+    lanes = -(-(width // groups) // 128) * 128
+    return members == 4 and groups * members * groups * share * lanes * 2 < 8 << 20
 
 
 def shards(
@@ -101,15 +390,16 @@
     base_own = (
         jnp.sum(states_own.astype(jnp.float32) * live_own[:, :, None], axis=1) / counted_own
     )
-    pooled_all = lax.all_gather(pooled, "dp", axis=0, tiled=True)
-    terms = lax.dot_general(
-        pooled_all, out_weight, (((1,), (1,)), ((), ())), preferred_element_type=jnp.float32
-    ).reshape(groups, members, share, -1)
-    mine = lax.psum_scatter(terms, "mp", scatter_dimension=1, tiled=True)
-    mine = mine.reshape(groups, share, -1)
-    swapped = lax.all_to_all(mine, "dp", 0, 0, tiled=True)
-    projected = jnp.swapaxes(swapped, 0, 1).reshape(share, width)
-    refreshed = (base_own + projected).astype(jnp.bfloat16)
+    block = width // groups
+    use_kernels = kernels_fit(groups, members, width, share)
+    if use_kernels:
+        base_blocks = jnp.swapaxes(base_own.reshape(share, groups, block), 0, 1)
+        gathered = tail(pooled, out_weight.T, base_blocks, groups, members)
+        refreshed_all = jnp.swapaxes(
+            gathered.reshape(groups * members, groups, share, block), 1, 2
+        ).reshape(groups * members * share, width)
+    else:
+        refreshed_all = gather_refreshed(pooled, out_weight, base_own, groups, members)
 
     root = math.sqrt(width)
     owned = label_table.shape[0]
@@ -121,13 +411,39 @@
     )
     kept = jnp.where(replaced, 0.0, balance)
     early_slopes, early_loss = focal(queries, label_table, positives, label_ids, kept, root)
-    query_part = jnp.dot(early_slopes, label_table, preferred_element_type=jnp.float32) / root
-    query_sum, loss_sum, summed_weight = lax.psum(
-        (query_part, early_loss, jnp.sum(balance)), ("dp", "mp")
-    )
-    new_ids = lax.all_gather(first_label + refresh_rows, ("dp", "mp"), axis=0, tiled=True)
-    new_balance = lax.all_gather(balance[refresh_rows], ("dp", "mp"), axis=0, tiled=True)
-    refreshed_all = lax.all_gather(refreshed, ("dp", "mp"), axis=0, tiled=True)
+    new_ids = first_label + refresh_rows
+    if use_kernels:
+        part = jnp.swapaxes(
+            (jnp.dot(early_slopes, label_table, preferred_element_type=jnp.float32) / root).reshape(
+                queries.shape[0], groups, block
+            ),
+            0,
+            1,
+        )
+        scalars = jnp.stack([early_loss, jnp.sum(balance)] + [jnp.float32(0)] * (share - 2))
+        meta = jnp.pad(
+            jnp.stack([new_ids.astype(jnp.float32), balance[refresh_rows], scalars]),
+            ((0, 5), (0, block - share)),
+        )
+        reduced = early_reduce(part, meta, groups, members)
+        rows = queries.shape[0] // members
+        query_sum = (
+            reduced[:, :rows]
+            .reshape(groups, members, rows, block)
+            .transpose(1, 2, 0, 3)
+            .reshape(queries.shape[0], width)
+        )
+        new_ids = reduced[:, rows, :share].reshape(-1).astype(jnp.int32)
+        new_balance = reduced[:, rows + 1, :share].reshape(-1)
+        loss_sum = jnp.sum(reduced[:, rows + 2, 0])
+        summed_weight = jnp.sum(reduced[:, rows + 2, 1])
+    else:
+        query_part = jnp.dot(early_slopes, label_table, preferred_element_type=jnp.float32) / root
+        query_sum, loss_sum, summed_weight = lax.psum(
+            (query_part, early_loss, jnp.sum(balance)), ("dp", "mp")
+        )
+        new_ids = lax.all_gather(new_ids, ("dp", "mp"), axis=0, tiled=True)
+        new_balance = lax.all_gather(balance[refresh_rows], ("dp", "mp"), axis=0, tiled=True)
     late_slopes, late_loss = focal(queries, refreshed_all, positives, new_ids, new_balance, root)
     query_late = jnp.dot(late_slopes, refreshed_all, preferred_element_type=jnp.float32) / root
     own_late = lax.dynamic_slice_in_dim(
@@ -144,6 +460,19 @@
     factor = total_labels / summed_weight
     loss = factor * (loss_sum + late_loss) / (queries.shape[0] * total_labels)
     return (factor * label_part, factor * (query_sum + query_late), loss)
+
+
+def gather_refreshed(pooled, out_weight, base_own, groups, members):
+    share, width = base_own.shape
+    pooled_all = lax.all_gather(pooled, "dp", axis=0, tiled=True)
+    terms = lax.dot_general(
+        pooled_all, out_weight, (((1,), (1,)), ((), ())), preferred_element_type=jnp.float32
+    ).reshape(groups, members, share, -1)
+    mine = lax.psum_scatter(terms, "mp", scatter_dimension=1, tiled=True)
+    swapped = lax.all_to_all(mine.reshape(groups, share, -1), "dp", 0, 0, tiled=True)
+    projected = jnp.swapaxes(swapped, 0, 1).reshape(share, width)
+    refreshed = (base_own + projected).astype(jnp.bfloat16)
+    return lax.all_gather(refreshed, ("dp", "mp"), axis=0, tiled=True)
 
 
 def balances(label_counts):

time: 445 us -> 257 us (0.58)
  waiting for transfers between devices: 258 us -> 29.5 us
  Pallas kernels: 0 us -> 121 us
  blocking collectives: 110 us -> 0 us
  local copies, waits for them, and re-layouts: 13 us -> 38.7 us
  other arithmetic: 15.6 us -> 21.6 us
  starting transfers between devices: 5.86 us -> 0.04 us
    pallas_call x0 -> x2, Pallas kernels: none -> 121 us  [the longest x1 72.5 us: early_reduce(): pl.pallas_call(functools.partial(early_kernel, groups, members), out_shap...]
    psum x1 -> x0, waiting for transfers between devices: 97.6 us -> none  [shards(): lax.psum((query_part, early_loss, jnp.sum(balance)), ('dp', 'mp'))]
    all_gather x1, waiting for transfers between devices: 124 us -> 29.5 us  [shards(): lax.all_gather(jnp.concatenate([q_weight, key_matrix, value_matrix], axis...]
    unnamed x2 -> x0, blocking collectives: 78.6 us -> none
    all_gather x1 -> x0, blocking collectives: 31.3 us -> none  [shards(): pooled_all = lax.all_gather(pooled, 'dp', axis=0, tiled=True)]
    unnamed x5 -> x1, waiting for transfers between devices: 31 us -> 0.02 us
    reshape x2 -> x4, local copies, waits for them, and re-layouts: 2.32 us -> 12.7 us  [the longest x1 4.68 us: shards(): refreshed_all = jnp.swapaxes(gathered.reshape(groups * members, groups, s...]
    all_to_all x1 -> x0, starting transfers between devices: 5.52 us -> none  [shards(): swapped = lax.all_to_all(mine, 'dp', 0, 0, tiled=True)]
  transfers between devices with their start and end apart: 5 -> 1, of which waited for: 4 -> 1; matrix products, arithmetic and copies ran while one was open for 4% -> 15% of each run, Pallas kernels for 0% -> 28%
where the time goes in v2:
time: 257 us; the launch traced here: 256 us
  Pallas kernels  121 us (47%)
  local copies, waits for them, and re-layouts  38.7 us (15%)
  waiting for transfers between devices  29.5 us (11%)
  matrix products  26.9 us (10%)
  other arithmetic  21.6 us (8%)
  between operations  17.5 us (7%)
    pallas_call x1, Pallas kernels, early_reduce(): pl.pallas_call(functools.partial(early_kernel, groups, members), out_shap...  72.5 us
    pallas_call x1, Pallas kernels, tail(): pl.pallas_call(functools.partial(tail_kernel, groups, members), out_shape...  49 us
    all_gather x1, waiting for transfers between devices, shards(): lax.all_gather(jnp.concatenate([q_weight, key_matrix, value_matrix], axis...  29.5 us
    dot_general x1, matrix products, shards(): raw = jnp.dot(normed, weights, preferred_element_type=jnp.float32)  9.41 us
    dot_general x2, matrix products, focal(): lax.dot_general(queries, table, (((1,), (1,)), ((), ())), preferred_eleme...  5.7 us
  transfers between devices with their start and end apart: 1, of which 1 were waited for; matrix products, arithmetic and copies ran while one was open for 15% of the time, Pallas kernels for 28%

profile of v2, /device:TPU:0, one launch (start us, length us, event | category | flops | bytes accessed | tf_op | source)
XLA Modules:
  0.0 255.8 jit_solution(10474715985340493984)
XLA Ops:
  7.2 0.0 all-gather.2.cloned.1.call-start
  7.2 2.5 pad_maximum_fusion
  9.8 0.5 convert_reduce_fusion.1
  10.3 0.7 copy.44
  11.0 0.7 copy.47
  11.7 0.6 fusion.35
  12.3 0.1 copy.49
  12.3 1.6 fusion.10
  14.0 0.7 reduce_sum.114
  14.7 0.7 copy.48
  15.4 0.8 copy.41
  16.2 0.7 convert_bitcast_fusion
  16.9 1.3 fusion.36
  18.2 0.6 gather_fusion
  18.9 0.7 fusion.34
  19.6 0.4 compare_reduce_fusion.1
  20.0 2.7 %fusion.27 = (f32[]{:T(128)}, bf16[128,256]{1,0:T(8,128)(2,1)S(1)}) fusion(f32[256]{0:T(256)S(1)} %broadcast_select_fusion, pred[128,256]{1,0:T(8,128)(4,1)S(1)} %compare_reduce_fusion.1, bf16[128,3584]{1,0:T(8,128)(2,1)} %param.22, bf16[256,3584]{1,0:T(8,128)(2,1)S(1)} %copy-done), kind=kOutput, calls=%fused_computation.56 | convolution fusion | flops 235765760 | bytes 2851844 | tf_op jit(solution)/shard_map/dot_general | solution.py:486
  22.8 0.1 copy.53
  22.9 1.7 convolution_multiply_fusion.2
  24.6 2.8 %copy.42 = f32[128,3584]{0,1:T(8,128)} copy(f32[128,3584]{1,0:T(8,128)} %convolution_multiply_fusion.2) | data formatting | bytes 3670016 | tf_op jit(solution)/shard_map/div | solution.py:417
  27.4 2.8 %copy.43 = f32[128,8,448]{2,0,1:T(8,128)} copy(f32[128,8,448]{0,2,1:T(8,128)} %bitcast.104) | data formatting | bytes 3670016 | tf_op jit(solution)/shard_map/reshape | solution.py:417
  30.2 1.3 maximum_bitcast_fusion
  31.5 1.6 copy-done.2
  33.1 72.5 %early_reduce.1 = f32[32,40,448]{2,1,0:T(8,128)S(1)} custom-call(f32[8,128,448]{2,1,0:T(8,128)S(1)} %bitcast.96, f32[8,448]{1,0:T(8,128)S(1)} %select_maximum_fusion.meta), custom_call_target="tpu_custom_call" | custom-call | tf_op jit(solution)/shard_map/early_reduce/pallas_call | solution.py:202
  105.6 1.7 slice.47
  107.4 0.5 copy-done.1
  107.8 0.1 convert_reduce_fusion
  107.9 0.1 convert_element_type.72
  108.0 1.0 slice_reduce_fusion.2
  108.9 0.1 mul.260
  109.0 4.2 %copy.55 = f32[4,32,8,448]{3,2,1,0:T(8,128)} copy(f32[4,32,8,448]{3,1,0,2:T(8,128)} %bitcast.99) | data formatting | bytes 3670016 | tf_op jit(solution)/shard_map/transpose | solution.py:433
  113.2 3.0 %reshape.166 = f32[128,3584]{1,0:T(8,128)} reshape(f32[4,32,8,448]{3,2,1,0:T(8,128)} %copy.55) | data formatting | bytes 3670016 | tf_op jit(solution)/shard_map/reshape | solution.py:434
  116.2 1.7 slice_reduce_fusion
  118.7 0.1 fusion.33
  118.8 0.1 pad_maximum_fusion.1
  118.8 0.4 compare_reduce_fusion
  119.2 2.9 %fusion = f32[512]{0:T(512)S(1)} fusion(bf16[512,3584]{1,0:T(8,128)(2,1)} %param.12), kind=kLoop, calls=%fused_computation.4 | loop fusion | flops 5504512 | bytes 3672064 | tf_op jit(solution)/shard_map/reduce_sum | solution.py:352
  122.1 0.1 broadcast_and_fusion
  122.3 0.1 fusion.30.base
  122.4 29.5 %all-gather.2.cloned.1.call-done = bf16[3584,1152]{1,0:T(8,128)(2,1)} async-done(((bf16[448,1152]{1,0:T(8,128)(2,1)}), bf16[3584,1152]{1,0:T(8,128)(2,1)}) %all-gather.2.cloned.1.call-update) | async-done | bytes 8257552 | tf_op jit(solution)/shard_map/all_gather | solution.py:356
  151.9 9.4 %fusion.5 = f32[512,1152]{1,0:T(8,128)S(1)} fusion(bf16[3584,1152]{1,0:T(8,128)(2,1)} %all-gather.2.cloned.1.call-done, bf16[512,3584]{1,0:T(8,128)(2,1)} %param.12, f32[3584]{0:T(1024)S(1)} %copy-done.13, f32[512]{0:T(512)S(1)} %add_rsqrt_fusion), kind=kOutput, calls=%fused_computation.12 | convolution fusion | flops 4235198464 | bytes 14303232 | tf_op jit(solution)/shard_map/dot_general | solution.py:359
  161.3 1.4 slice.55
  162.7 0.6 copy-done.3
  163.3 2.7 %reshape.160 = f32[32,16,7,128]{3,2,1,0:T(8,128)} reshape(f32[512,896]{1,0:T(8,128)} %slice.55) | data formatting | bytes 3670016 | tf_op jit(solution)/shard_map/reshape | solution.py:364
  166.0 3.1 %slice_negate_fusion = (f32[32,16,7,64]{3,2,1,0:T(8,128)S(1)}, f32[32,16,7,64]{3,2,1,0:T(8,128)S(1)}) fusion(f32[32,16,7,128]{3,2,1,0:T(8,128)} %reshape.160), kind=kLoop, calls=%fused_computation.15 | loop fusion | flops 229376 | bytes 3670016 | tf_op jit(solution)/shard_map/neg | solution.py:28
  169.1 0.6 maximum_multiply_fusion
  169.7 0.2 mul.277
  170.0 0.8 copy-done.4
  170.8 1.6 fusion.9
  172.4 2.9 %reshape.161 = bf16[32,16,7,128]{3,2,1,0:T(8,128)(2,1)} reshape(bf16[512,896]{1,0:T(8,128)(2,1)} %fusion.9) | data formatting | bytes 1835008 | tf_op jit(solution)/shard_map/reshape.8
  175.3 0.1 slice_negate_fusion.1
  175.5 1.1 fusion.21
  176.6 3.3 %fusion.37 = (f32[32,7,16]{2,1,0:T(8,128)S(1)}, f32[32,1,7,16,16]{3,4,2,0,1:T(8,128)S(1)}) fusion(bf16[32,16,128,1]{2,1,3,0:T(8,128)(2,1)S(1)} %bitcast.107, bf16[32,16,7,128]{3,2,1,0:T(8,128)(2,1)} %reshape.161, pred[32,16,16]{1,2,0:T(8,128)(4,1)S(1)} %broadcast_and_fusion), kind=kOutput, calls=%fused_computation.98 | convolution fusion | flops 14848512 | bytes 1300480 | tf_op jit(solution)/shard_map/ntgrd,nsgd->ngrts/dot_general | solution.py:39
  179.9 0.7 fusion.11
  180.5 0.1 fusion.31.pooled
  180.6 49.0 %tail.1 = bf16[32,64,448]{2,1,0:T(8,128)(2,1)S(1)} custom-call(bf16[32,896]{1,0:T(8,128)(2,1)S(1)} %fusion.31.pooled, bf16[896,448]{1,0:T(8,128)(2,1)S(1)} %bitcast.98, f32[8,8,448]{2,1,0:T(8,128)S(1)} %fusion.30.base), custom_call_target="tpu_custom_call" | custom-call | tf_op jit(solution)/shard_map/tail/pallas_call | solution.py:307
  229.6 2.2 copy.74
  231.8 4.7 %reshape.164 = bf16[256,3584]{1,0:T(8,128)(2,1)} reshape(bf16[32,8,8,448]{3,2,1,0:T(8,128)(2,1)} %bitcast.102) | data formatting | bytes 3670016 | tf_op jit(solution)/shard_map/reshape | solution.py:400
  236.5 3.0 %fusion.29 = (f32[]{:T(128)}, bf16[128,256]{1,0:T(8,128)(2,1)S(1)}) fusion(f32[256]{0:T(256)S(1)} %mul.260, pred[128,256]{1,0:T(8,128)(4,1)S(1)} %compare_reduce_fusion, bf16[256,3584]{1,0:T(8,128)(2,1)} %reshape.164, bf16[128,3584]{1,0:T(8,128)(2,1)S(1)} %copy-done.5), kind=kOutput, calls=%fused_computation.58 | convolution fusion | flops 235765760 | bytes 2851844 | tf_op jit(solution)/shard_map/dot_general | solution.py:486
  240.7 3.7 %fusion.4 = f32[128,3584]{1,0:T(8,128)} fusion(f32[128,3584]{1,0:T(8,128)} %reshape.166, bf16[128,256]{1,0:T(8,128)(2,1)S(1)} %get-tuple-element.16, bf16[256,3584]{1,0:T(8,128)(2,1)} %reshape.164, f32[]{:T(128)S(6)} %div.111), kind=kOutput, calls=%fused_computation.10 | convolution fusion | flops 236257280 | bytes 5570564 | tf_op jit(solution)/shard_map/dot_general | solution.py:448
  244.5 0.1 dynamic-slice_bitcast_fusion
  244.5 0.1 copy.54
  244.6 0.7 scatter_fusion
  245.3 2.5 convolution_multiply_fusion
  (38 shorter events, 0.2 us)
Async XLA Ops:
  7.2 12.9 %copy-start = (bf16[256,3584]{1,0:T(8,128)(2,1)S(1)}, bf16[256,3584]{1,0:T(8,128)(2,1)}, u32[]{:S(2)}) copy-start(bf16[256,3584]{1,0:T(8,128)(2,1)} %param.19) | copy-start | bytes 5505028
  7.2 2.6 %copy-start.10 = (s32[32,16]{0,1:T(8,128)S(1)}, s32[32,16]{0,1:T(8,128)}, u32[]{:S(2)}) copy-start(s32[32,16]{0,1:T(8,128)} %param.13) | copy-start | bytes 6148
  7.2 7.5 %copy-start.6 = (bf16[448,896]{1,0:T(8,128)(2,1)S(1)}, bf16[448,896]{1,0:T(8,128)(2,1)}, u32[]{:S(2)}) copy-start(bf16[448,896]{1,0:T(8,128)(2,1)} %param.18) | copy-start | bytes 2408452
  7.2 144.7 %all-gather.2.cloned.1.call-start = ((), (), s32[]{:S(2)}) async-start(), calls=%async_computation | async-start | bytes 9289728 | tf_op jit(solution)/shard_map/all_gather | solution.py:356
  31.5 1.6 copy-start.2
  105.6 2.2 copy-start.1
  116.2 5.9 %copy-start.8 = (pred[32,16]{1,0:T(8,128)(4,1)S(1)}, pred[32,16]{1,0:T(8,128)(4,1)}, u32[]{:S(2)}) copy-start(pred[32,16]{1,0:T(8,128)(4,1)} %copy.44) | copy-start | bytes 1540
  116.2 6.0 %copy-start.7 = (f32[8,8,448]{2,1,0:T(8,128)S(1)}, f32[8,8,448]{2,1,0:T(8,128)}, u32[]{:S(2)}) copy-start(f32[8,8,448]{2,1,0:T(8,128)} %reduce_sum.114) | copy-start | bytes 344068
  116.2 6.0 %copy-start.11 = (f32[8]{0:T(128)S(1)}, f32[8]{0:T(128)}, u32[]{:S(2)}) copy-start(f32[8]{0:T(128)} %get-tuple-element.5) | copy-start | bytes 100
  118.7 33.1 %copy-start.13 = (f32[3584]{0:T(1024)S(1)}, f32[3584]{0:T(1024)}, u32[]{:S(2)}) copy-start(f32[3584]{0:T(1024)} %param.14) | copy-start | bytes 43012
  161.3 2.0 copy-start.3
  169.1 1.7 copy-start.4
  172.4 2.9 %slice-start = ((f32[512,1152]{1,0:T(8,128)}), f32[512,128]{1,0:T(8,128)S(1)}, s32[]{:S(2)}) async-start(f32[512,1152]{1,0:T(8,128)} %copy-done.3), calls=%async_computation.1 | async-start | bytes 524288 | tf_op jit(solution)/shard_map/slice | solution.py:361
  175.4 4.4 %copy-start.9 = (f32[32,16]{1,0:T(8,128)S(1)}, f32[32,16]{1,0:T(8,128)}, u32[]{:S(2)}) copy-start(f32[32,16]{1,0:T(8,128)} %copy.47) | copy-start | bytes 6148
  179.8 0.7 copy-start.12
  231.8 4.7 %copy-start.5 = (bf16[128,3584]{1,0:T(8,128)(2,1)S(1)}, bf16[128,3584]{1,0:T(8,128)(2,1)}, u32[]{:S(2)}) copy-start(bf16[128,3584]{1,0:T(8,128)(2,1)} %param.22) | copy-start | bytes 2752516
Sparse Core Ops, SparseCore 0:
  10.2 141.5 all-gather.1

commit v3 on v2

--- a/solution.py
+++ b/solution.py
@@ -9,6 +9,7 @@
 from jax.sharding import PartitionSpec as P
 
 MESH = pl.DeviceIdType.MESH
+SIDES = 2
 
 HEAD_WIDTH = 128
 
@@ -107,12 +108,17 @@
         slot = group * members + member
         copy(group, slot, group_sem, step, (lax.rem(group + step, groups), member)).wait_send()
 
-    each(1, groups, send)
-    forward(group)
-    each(1, groups, pass_on)
-    each(0, groups, relay)
-    each(0, groups, finish)
-    each(1, groups, sent)
+    def start():
+        each(1, groups, send)
+        forward(group)
+
+    def end():
+        each(1, groups, pass_on)
+        each(0, groups, relay)
+        each(0, groups, finish)
+        each(1, groups, sent)
+
+    return start, end
 
 
 def spread_sems(groups, members):
@@ -125,12 +131,46 @@
     ]
 
 
-def early_kernel(
-    groups, members, part, meta, blocks, got, sums, terms, s1, r1, s2, r2, *sems
+def project_kernel(
+    groups,
+    members,
+    states,
+    gain,
+    q_weight,
+    key_matrix,
+    value_matrix,
+    queries,
+    table,
+    positives,
+    label_ids,
+    kept,
+    meta,
+    raw,
+    slopes,
+    blocks,
+    weights,
+    normed,
+    part,
+    got,
+    sums,
+    terms,
+    up_sem,
+    down_sem,
+    side_sem,
+    landed,
+    s1,
+    r1,
+    s2,
+    r2,
+    *sems,
 ):
     group, member = lax.axis_index("dp"), lax.axis_index("mp")
     own = group * members + member
-    rows = part.shape[1] // members
+    depth = groups // SIDES
+    level, side = group // SIDES, lax.rem(group, SIDES)
+    block = table.shape[1] // groups
+    rows = queries.shape[0] // members
+    heads, kv = q_weight.shape[1], key_matrix.shape[1]
     barrier = pltpu.get_barrier_semaphore()
 
     def greet_member(step):
@@ -143,7 +183,132 @@
 
     each(1, members, greet_member)
     each(1, groups, greet_group)
+    weights[group, :, :heads] = q_weight[...]
+    weights[group, :, heads : heads + kv] = key_matrix[...]
+    weights[group, :, heads + kv :] = value_matrix[...]
     pl.semaphore_wait(barrier, groups + members - 2)
+
+    def weight_copy(slot, sem, peer):
+        return remote(
+            weights.at[slot], weights.at[slot], sem.at[slot], landed.at[slot], (peer, member)
+        )
+
+    def up(slot):
+        return weight_copy(slot, up_sem, group + SIDES)
+
+    def down(slot):
+        return weight_copy(slot, down_sem, group - SIDES)
+
+    def across(slot):
+        return weight_copy(slot, side_sem, level * SIDES + 1 - side)
+
+    def travel(step):
+        @pl.when(level >= step)
+        def _():
+            slot = group - step * SIDES
+            if step > 0:
+                weight_copy(slot, down_sem, group - SIDES).wait_recv()
+
+            @pl.when(level < depth - 1)
+            def _():
+                up(slot).start()
+
+            across(slot).start()
+
+        if step == 0:
+
+            @pl.when(level > 0)
+            def _():
+                down(group).start()
+
+        else:
+
+            @pl.when(level + step < depth)
+            def _():
+                slot = group + step * SIDES
+                weight_copy(slot, up_sem, group + SIDES).wait_recv()
+
+                @pl.when(level > 0)
+                def _():
+                    down(slot).start()
+
+                across(slot).start()
+
+    tokens = states.shape[0]
+    tile = 128 if tokens % 128 == 0 else tokens
+
+    def multiply(slot):
+        def some(index):
+            at = pl.ds(pl.multiple_of(index * tile, tile), tile)
+            raw[at, :] += jnp.dot(
+                normed[slot, at, :], weights[slot], preferred_element_type=jnp.float32
+            )
+
+        each(0, tokens // tile, some)
+
+    def multiply_step(step):
+        @pl.when(level >= step)
+        def _():
+            multiply(group - step * SIDES)
+
+        if step > 0:
+
+            @pl.when(level + step < depth)
+            def _():
+                multiply(group + step * SIDES)
+
+    def multiply_across(step):
+        def one(at):
+            slot = at * SIDES + 1 - side
+            across(slot).wait_recv()
+            multiply(slot)
+
+        @pl.when(level >= step)
+        def _():
+            one(level - step)
+
+        if step > 0:
+
+            @pl.when(level + step < depth)
+            def _():
+                one(level + step)
+
+    travel(0)
+
+    root = math.sqrt(table.shape[1])
+    logits = (
+        lax.dot_general(
+            queries[...],
+            table[...],
+            (((1,), (1,)), ((), ())),
+            preferred_element_type=jnp.float32,
+        )
+        / root
+    )
+    matched = positives[:, 0:1] == label_ids[...]
+    for index in range(1, positives.shape[1]):
+        matched = matched | (positives[:, index : index + 1] == label_ids[...])
+    signs = jnp.where(matched, 1.0, -1.0)
+    margin = signs * logits
+    small = jnp.exp(-jnp.abs(margin))
+    larger, smaller = 1.0 / (1.0 + small), small / (1.0 + small)
+    missed = jnp.where(margin >= 0.0, smaller, larger)
+    hit = jnp.where(margin >= 0.0, larger, smaller)
+    softened = jnp.maximum(-margin, 0.0) + jnp.log1p(small)
+    loss = jnp.sum(kept[...] * missed * missed * softened)
+    early = (
+        kept[...] * signs * (-(missed * missed) * (2.0 * hit * softened + missed))
+    ).astype(jnp.bfloat16)
+    slopes[...] = early
+    for at in range(groups):
+        part[at] = (
+            jnp.dot(
+                early,
+                table[:, at * block : (at + 1) * block],
+                preferred_element_type=jnp.float32,
+            )
+            / root
+        )
 
     def member_copy(step):
         peer = lax.rem(member + step, members)
@@ -163,6 +328,19 @@
         ).wait_recv()
 
     each(1, members, lambda step: member_copy(step).start())
+
+    def normalize(index):
+        at = pl.ds(pl.multiple_of(index * 64, 64), 64)
+        wide = states[at, :].astype(jnp.float32)
+        scaled = lax.rsqrt(jnp.mean(wide * wide, axis=1, keepdims=True) + norm_eps)
+        ready = (wide * scaled * gain[...]).astype(jnp.bfloat16)
+        for piece in range(groups):
+            normed[piece, at, :] = ready[:, piece * block : (piece + 1) * block]
+
+    each(0, tokens // 64, normalize)
+    raw[...] = jnp.zeros_like(raw)
+    multiply_step(0)
+    travel(1)
     each(1, members, member_wait)
     first = pl.multiple_of(member * rows, rows)
 
@@ -185,42 +363,106 @@
         ).wait_recv()
 
     each(1, groups, lambda step: group_copy(step).start())
+    multiply_step(1)
+    multiply_across(0)
+    travel(2)
     each(1, groups, group_wait)
     total = sums[group]
     for step in range(1, groups):
         total = total + terms[lax.rem(group + step, groups)]
     blocks[own, :rows] = total
-    blocks[own, rows:] = meta[...]
-    spread(groups, members, blocks, *sems)
+    line = lax.broadcasted_iota(jnp.int32, meta.shape, 0)
+    blocks[own, rows:] = jnp.where(line == 3, loss, meta[...])
+    start, end = spread(groups, members, blocks, *sems)
+    start()
+    multiply_step(2)
+    multiply_across(1)
+    for step in range(3, depth):
+        travel(step)
+        multiply_step(step)
+    end()
+    for step in range(2, depth):
+        multiply_across(step)
+
     each(1, members, lambda step: member_copy(step).wait_send())
     each(1, groups, lambda step: group_copy(step).wait_send())
 
-
-def early_reduce(part, meta, groups, members):
-    _, batch, block = part.shape
-    rows = batch // members
+    def weights_sent(at):
+        slot = at * SIDES + side
+        across(slot).wait_send()
+
+        @pl.when((at <= level) & (level < depth - 1))
+        def _():
+            up(slot).wait_send()
+
+        @pl.when((at >= level) & (level > 0))
+        def _():
+            down(slot).wait_send()
+
+    each(0, depth, weights_sent)
+
+
+def project(
+    states,
+    gain,
+    q_weight,
+    key_matrix,
+    value_matrix,
+    queries,
+    table,
+    positives,
+    label_ids,
+    kept,
+    meta,
+    groups,
+    members,
+):
+    tokens, width = states.shape
+    batch = queries.shape[0]
+    rows, block = batch // members, width // groups
+    columns = q_weight.shape[1] + key_matrix.shape[1] + value_matrix.shape[1]
+    group_sems = [pltpu.SemaphoreType.DMA((groups,))]
     return pl.pallas_call(
-        functools.partial(early_kernel, groups, members),
-        out_shape=jax.ShapeDtypeStruct(
-            (groups * members, rows + meta.shape[0], block), jnp.float32
+        functools.partial(project_kernel, groups, members),
+        out_shape=(
+            jax.ShapeDtypeStruct((tokens, columns), jnp.float32),
+            jax.ShapeDtypeStruct((batch, table.shape[0]), jnp.bfloat16),
+            jax.ShapeDtypeStruct(
+                (groups * members, rows + meta.shape[0], block), jnp.float32
+            ),
         ),
-        in_specs=[pl.BlockSpec(memory_space=pltpu.VMEM)] * 2,
-        out_specs=pl.BlockSpec(memory_space=pltpu.VMEM),
+        in_specs=[pl.BlockSpec(memory_space=pltpu.VMEM)] * 11,
+        out_specs=tuple([pl.BlockSpec(memory_space=pltpu.VMEM)] * 3),
         scratch_shapes=[
+            pltpu.VMEM((groups, block, columns), jnp.bfloat16),
+            pltpu.VMEM((groups, tokens, block), jnp.bfloat16),
+            pltpu.VMEM((groups, batch, block), jnp.float32),
             pltpu.VMEM((members, groups, rows, block), jnp.float32),
             pltpu.VMEM((groups, rows, block), jnp.float32),
             pltpu.VMEM((groups, rows, block), jnp.float32),
+            *(group_sems * 4),
             pltpu.SemaphoreType.DMA((members,)),
             pltpu.SemaphoreType.DMA((members,)),
-            pltpu.SemaphoreType.DMA((groups,)),
-            pltpu.SemaphoreType.DMA((groups,)),
+            *(group_sems * 2),
             *spread_sems(groups, members),
         ],
         compiler_params=pltpu.CompilerParams(
-            collective_id=0, has_side_effects=True, vmem_limit_bytes=24 << 20
+            collective_id=0, has_side_effects=True, vmem_limit_bytes=48 << 20
         ),
-        name="early_reduce",
-    )(part, meta)
+        name="project",
+    )(
+        states,
+        gain,
+        q_weight,
+        key_matrix,
+        value_matrix,
+        queries,
+        table,
+        positives,
+        label_ids,
+        kept,
+        meta,
+    )
 
 
 def tail_kernel(
@@ -289,7 +531,9 @@
             total = total + parts[at * members + index]
         rows.append(total)
     blocks[own] = jnp.concatenate(rows, axis=0).astype(jnp.bfloat16)
-    spread(groups, members, blocks, *sems)
+    start, end = spread(groups, members, blocks, *sems)
+    start()
+    end()
     each(1, groups, lambda step: pool_copy(step).wait_send())
 
     def part_sent(step):
@@ -328,7 +572,7 @@
 
 def kernels_fit(groups, members, width, share):
     lanes = -(-(width // groups) // 128) * 128
-    return members == 4 and groups * members * groups * share * lanes * 2 < 8 << 20
+    return members == 4 and groups % SIDES == 0 and groups * members * groups * share * lanes * 2 < 8 << 20
 
 
 def shards(
@@ -348,15 +592,75 @@
     width = hidden_states.shape[1]
     group_tokens = hidden_states.shape[0]
     texts, length = token_ids.shape
-    states = hidden_states.astype(jnp.float32)
-    scaled = lax.rsqrt(jnp.mean(states * states, axis=1, keepdims=True) + norm_eps)
-    normed = (states * scaled * norm_gain).astype(jnp.bfloat16)
+    groups = lax.axis_size("dp")
+    members = lax.axis_size("mp")
+    share = texts // members
+    member = lax.axis_index("mp")
     heads = q_weight.shape[1]
     kv = key_matrix.shape[1]
-    weights = lax.all_gather(
-        jnp.concatenate([q_weight, key_matrix, value_matrix], axis=1), "dp", axis=0, tiled=True
-    )
-    raw = jnp.dot(normed, weights, preferred_element_type=jnp.float32)
+    block = width // groups
+    use_kernels = kernels_fit(groups, members, width, share)
+    root = math.sqrt(width)
+    owned = label_table.shape[0]
+    first_label = (lax.axis_index("dp") * members + member) * owned
+    label_ids = first_label + jnp.arange(owned, dtype=jnp.int32)
+    balance = balances(label_counts)
+    replaced = jnp.any(
+        refresh_rows[:, None] == jnp.arange(owned, dtype=jnp.int32)[None, :], axis=0
+    )
+    kept = jnp.where(replaced, 0.0, balance)
+    new_ids = first_label + refresh_rows
+    new_balance = balances(label_counts[refresh_rows])
+    if use_kernels:
+        sums = jnp.broadcast_to(jnp.sum(balance), (share,))
+        meta = jnp.pad(
+            jnp.stack([new_ids.astype(jnp.float32), new_balance, sums]),
+            ((0, 5), (0, block - share)),
+        )
+        raw, early_slopes, reduced = project(
+            hidden_states,
+            norm_gain[None, :],
+            q_weight,
+            key_matrix,
+            value_matrix,
+            queries,
+            label_table,
+            positives,
+            label_ids[None, :],
+            kept[None, :],
+            meta,
+            groups,
+            members,
+        )
+        rows = queries.shape[0] // members
+        query_sum = (
+            reduced[:, :rows]
+            .reshape(groups, members, rows, block)
+            .transpose(1, 2, 0, 3)
+            .reshape(queries.shape[0], width)
+        )
+        new_ids = reduced[:, rows, :share].reshape(-1).astype(jnp.int32)
+        new_balance = reduced[:, rows + 1, :share].reshape(-1)
+        summed_weight = jnp.sum(reduced[:, rows + 2, 0])
+        loss_sum = jnp.sum(reduced[:, rows + 3, 0])
+    else:
+        states = hidden_states.astype(jnp.float32)
+        scaled = lax.rsqrt(jnp.mean(states * states, axis=1, keepdims=True) + norm_eps)
+        normed = (states * scaled * norm_gain).astype(jnp.bfloat16)
+        weights = lax.all_gather(
+            jnp.concatenate([q_weight, key_matrix, value_matrix], axis=1),
+            "dp",
+            axis=0,
+            tiled=True,
+        )
+        raw = jnp.dot(normed, weights, preferred_element_type=jnp.float32)
+        early_slopes, early_loss = focal(queries, label_table, positives, label_ids, kept, root)
+        query_part = jnp.dot(early_slopes, label_table, preferred_element_type=jnp.float32) / root
+        query_sum, loss_sum, summed_weight = lax.psum(
+            (query_part, early_loss, jnp.sum(balance)), ("dp", "mp")
+        )
+        new_ids = lax.all_gather(new_ids, ("dp", "mp"), axis=0, tiled=True)
+        new_balance = lax.all_gather(new_balance, ("dp", "mp"), axis=0, tiled=True)
     query_raw = raw[:, :heads]
     key_raw = raw[:, heads : heads + kv]
     value_raw = raw[:, heads + kv :]
@@ -378,10 +682,6 @@
         jnp.sum(attended.astype(jnp.float32).reshape(texts, length, -1) * live[:, :, None], axis=1)
         / counted
     ).astype(jnp.bfloat16)
-    groups = lax.axis_size("dp")
-    members = lax.axis_size("mp")
-    share = texts // members
-    member = lax.axis_index("mp")
     live_own = lax.dynamic_slice_in_dim(live, member * share, share, 0)
     states_own = lax.dynamic_slice_in_dim(
         hidden_states, member * share * length, share * length, 0
@@ -390,8 +690,6 @@
     base_own = (
         jnp.sum(states_own.astype(jnp.float32) * live_own[:, :, None], axis=1) / counted_own
     )
-    block = width // groups
-    use_kernels = kernels_fit(groups, members, width, share)
     if use_kernels:
         base_blocks = jnp.swapaxes(base_own.reshape(share, groups, block), 0, 1)
         gathered = tail(pooled, out_weight.T, base_blocks, groups, members)
@@ -401,49 +699,6 @@
     else:
         refreshed_all = gather_refreshed(pooled, out_weight, base_own, groups, members)
 
-    root = math.sqrt(width)
-    owned = label_table.shape[0]
-    first_label = (lax.axis_index("dp") * members + member) * owned
-    label_ids = first_label + jnp.arange(owned, dtype=jnp.int32)
-    balance = balances(label_counts)
-    replaced = jnp.any(
-        refresh_rows[:, None] == jnp.arange(owned, dtype=jnp.int32)[None, :], axis=0
-    )
-    kept = jnp.where(replaced, 0.0, balance)
-    early_slopes, early_loss = focal(queries, label_table, positives, label_ids, kept, root)
-    new_ids = first_label + refresh_rows
-    if use_kernels:
-        part = jnp.swapaxes(
-            (jnp.dot(early_slopes, label_table, preferred_element_type=jnp.float32) / root).reshape(
-                queries.shape[0], groups, block
-            ),
-            0,
-            1,
-        )
-        scalars = jnp.stack([early_loss, jnp.sum(balance)] + [jnp.float32(0)] * (share - 2))
-        meta = jnp.pad(
-            jnp.stack([new_ids.astype(jnp.float32), balance[refresh_rows], scalars]),
-            ((0, 5), (0, block - share)),
-        )
-        reduced = early_reduce(part, meta, groups, members)
-        rows = queries.shape[0] // members
-        query_sum = (
-            reduced[:, :rows]
-            .reshape(groups, members, rows, block)
-            .transpose(1, 2, 0, 3)
-            .reshape(queries.shape[0], width)
-        )
-        new_ids = reduced[:, rows, :share].reshape(-1).astype(jnp.int32)
-        new_balance = reduced[:, rows + 1, :share].reshape(-1)
-        loss_sum = jnp.sum(reduced[:, rows + 2, 0])
-        summed_weight = jnp.sum(reduced[:, rows + 2, 1])
-    else:
-        query_part = jnp.dot(early_slopes, label_table, preferred_element_type=jnp.float32) / root
-        query_sum, loss_sum, summed_weight = lax.psum(
-            (query_part, early_loss, jnp.sum(balance)), ("dp", "mp")
-        )
-        new_ids = lax.all_gather(new_ids, ("dp", "mp"), axis=0, tiled=True)
-        new_balance = lax.all_gather(balance[refresh_rows], ("dp", "mp"), axis=0, tiled=True)
     late_slopes, late_loss = focal(queries, refreshed_all, positives, new_ids, new_balance, root)
     query_late = jnp.dot(late_slopes, refreshed_all, preferred_element_type=jnp.float32) / root
     own_late = lax.dynamic_slice_in_dim(

time: 257 us -> 239 us (0.930)
  Pallas kernels: 121 us -> 178 us
  waiting for transfers between devices: 29.5 us -> 0 us
  between operations: 17.5 us -> 3.99 us
  matrix products: 26.9 us -> 16 us
  other arithmetic: 21.6 us -> 11.3 us
  local copies, waits for them, and re-layouts: 38.7 us -> 29.2 us
    pallas_call x1, Pallas kernels: 72.5 us -> 121 us  [project(): pl.pallas_call(functools.partial(project_kernel, groups, members), out_sh...]
    all_gather x1 -> x0, waiting for transfers between devices: 29.5 us -> none  [shards(): lax.all_gather(jnp.concatenate([q_weight, key_matrix, value_matrix], axis...]
    dot_general x2 -> x0, matrix products: 11.1 us -> none  [the longest x1 9.41 us: shards(): raw = jnp.dot(normed, weights, preferred_element_type=jnp.float32)]
    pallas_call x1, Pallas kernels: 49 us -> 56.9 us  [tail(): pl.pallas_call(functools.partial(tail_kernel, groups, members), out_shape...]
    transpose x1, local copies, waits for them, and re-layouts: 4.22 us -> 1.22 us  [shards(): query_sum = reduced[:, :rows].reshape(groups, members, rows, block).trans...]
    unnamed x30 -> x24, local copies, waits for them, and re-layouts: 5 us -> 8 us
    reduce_sum x3 -> x2, other arithmetic: 5.89 us -> 2.94 us  [the longest x1 1.63 us: shards(): loss_sum = jnp.sum(reduced[:, rows + 3, 0])]
    dot_general x2 -> x1, matrix products: 5.7 us -> 2.86 us  [focal(): lax.dot_general(queries, table, (((1,), (1,)), ((), ())), preferred_eleme...]
  transfers between devices with their start and end apart: 1 -> 0, of which waited for: 1 -> 0; matrix products, arithmetic and copies ran while one was open for 15% -> 0% of each run, Pallas kernels for 28% -> 0%
where the time goes in v3:
time: 239 us; the launch traced here: 238 us
  Pallas kernels  178 us (74%)
  local copies, waits for them, and re-layouts  29.2 us (12%)
  matrix products  16 us (7%)
  other arithmetic  11.3 us (5%)
  between operations  3.99 us (2%)
    pallas_call x1, Pallas kernels, project(): pl.pallas_call(functools.partial(project_kernel, groups, members), out_sh...  121 us
    pallas_call x1, Pallas kernels, tail(): pl.pallas_call(functools.partial(tail_kernel, groups, members), out_shape...  56.9 us
    unnamed x24, local copies, waits for them, and re-layouts  8 us
    dot_general x1, matrix products, attend(): jnp.einsum('ntgrd,nsgd->ngrts', query_r, key_r, preferred_element_type=jn...  4.82 us

profile of v3, /device:TPU:0, one launch (start us, length us, event | category | flops | bytes accessed | tf_op | source)
XLA Modules:
  0.0 238.2 jit_solution(17214111359796236589)
XLA Ops:
  0.6 0.7 convert_bitcast_fusion
  1.3 1.3 gather_fusion
  2.7 0.0 copy-done.10
  2.7 1.3 fusion.27
  4.0 0.7 pad.15.clone
  4.7 0.1 maximum_maximum_fusion
  4.8 0.8 copy.37.positives
  5.6 0.7 fusion.22
  6.3 0.7 broadcast_in_dim.28.gain
  7.0 0.0 copy-start
  7.1 1.2 copy-done
  8.2 1.5 copy-done.2
  9.7 1.1 copy-done.3
  10.9 0.9 copy-done.4
  11.8 0.9 copy-done.5
  12.7 120.7 %project.1 = (f32[512,1152]{1,0:T(8,128)}, bf16[128,256]{1,0:T(8,128)(2,1)S(1)}, f32[32,40,448]{2,1,0:T(8,128)}) custom-call(bf16[512,3584]{1,0:T(8,128)(2,1)} %states.1, f32[1,3584]{1,0:T(1,128)S(1)} %broadcast_in_dim.28.gain, bf16[448,896]{1,0:T(8,128)(2,1)S(1)} %copy-done.3, bf16[448,128]{1,0:T(8,128)(2,1)S(1)} %copy-done.4, ...), custom_call_target="tpu_custom_call" | custom-call | tf_op jit(solution)/shard_map/project/pallas_call | solution.py:425
  133.3 2.8 %slice.43 = f32[512,896]{1,0:T(8,128)} slice(f32[512,1152]{1,0:T(8,128)} %get-tuple-element.8), slice={[0:512], [0:896]} | slice | bytes 3670016 | tf_op jit(solution)/shard_map/slice | solution.py:664
  136.2 1.6 reshape.173
  137.8 0.8 slice_negate_fusion
  138.6 0.1 fusion.21
  138.6 0.1 pad_maximum_fusion
  138.7 0.6 maximum_multiply_fusion
  139.3 0.2 mul.219
  139.6 0.8 copy-done.6
  140.4 1.0 fusion.2
  141.4 2.0 reshape.174
  143.4 0.1 slice_negate_fusion.1
  143.6 0.8 fusion.13
  144.4 0.0 copy-done.9
  144.4 0.1 copy.40
  144.5 0.1 broadcast_and_fusion
  144.6 0.0 copy-done.7
  144.6 4.8 %fusion.28 = (f32[32,7,16]{2,1,0:T(8,128)}, f32[32,1,7,16,16]{3,4,2,0,1:T(8,128)}) fusion(bf16[32,16,128,1]{2,1,3,0:T(8,128)(2,1)} %bitcast.99, bf16[32,16,7,128]{3,2,1,0:T(8,128)(2,1)S(1)} %copy-done.7, pred[32,16,16]{1,2,0:T(8,128)(4,1)S(1)} %broadcast_and_fusion), kind=kOutput, calls=%fused_computation.75 | convolution fusion | flops 14848512 | bytes 1300480 | tf_op jit(solution)/shard_map/ntgrd,nsgd->ngrts/dot_general | solution.py:40
  149.5 0.1 copy.43
  149.6 2.2 fusion.4
  151.7 0.0 copy-start.8
  151.7 0.1 fusion.19.pooled
  151.8 0.1 fusion.26
  151.9 0.1 copy.45
  152.0 1.6 fusion.3
  153.6 0.1 reduce_sum.94
  153.7 0.1 fusion.18.base
  153.8 0.0 copy-done.8
  153.8 0.8 copy.44
  154.6 56.9 %tail.1 = bf16[32,64,448]{2,1,0:T(8,128)(2,1)S(1)} custom-call(bf16[32,896]{1,0:T(8,128)(2,1)S(1)} %fusion.19.pooled, bf16[896,448]{1,0:T(8,128)(2,1)S(1)} %bitcast.90, f32[8,8,448]{2,1,0:T(8,128)S(1)} %fusion.18.base), custom_call_target="tpu_custom_call" | custom-call | tf_op jit(solution)/shard_map/tail/pallas_call | solution.py:551
  211.5 0.9 copy.67
  212.4 0.0 copy-start.1
  212.4 3.3 %reshape.177 = bf16[256,3584]{1,0:T(8,128)(2,1)} reshape(bf16[32,8,8,448]{3,2,1,0:T(8,128)(2,1)S(1)} %bitcast.94) | data formatting | bytes 3670016 | tf_op jit(solution)/shard_map/reshape | solution.py:698
  215.7 1.0 convert_reduce_fusion
  216.7 0.1 convert_element_type.74
  216.8 0.4 compare_reduce_fusion
  217.2 0.1 copy.39
  217.3 1.0 slice_reduce_fusion.2
  218.2 0.1 mul.207
  218.3 0.0 copy-done.1
  218.3 2.9 %fusion.17 = (f32[]{:T(128)}, bf16[128,256]{0,1:T(8,128)(2,1)S(1)}) fusion(f32[256]{0:T(256)S(1)} %mul.207, pred[128,256]{0,1:T(32,128)(4,1)S(1)} %copy.39, bf16[256,3584]{1,0:T(8,128)(2,1)} %reshape.177, bf16[128,3584]{1,0:T(8,128)(2,1)S(1)} %copy-done.1), kind=kOutput, calls=%fused_computation.38 | convolution fusion | flops 235765760 | bytes 2851844 | tf_op jit(solution)/shard_map/dot_general | solution.py:741
  221.2 1.6 slice_reduce_fusion
  223.5 1.8 slice.47
  225.3 1.2 copy.49
  226.5 2.1 reshape.179
  228.6 3.7 %fusion.1 = f32[128,3584]{1,0:T(8,128)} fusion(f32[128,3584]{1,0:T(8,128)} %reshape.179, bf16[128,256]{0,1:T(8,128)(2,1)S(1)} %get-tuple-element.22, bf16[256,3584]{1,0:T(8,128)(2,1)} %reshape.177, f32[]{:T(128)S(6)} %div.105), kind=kOutput, calls=%fused_computation.5 | convolution fusion | flops 236257280 | bytes 5570564 | tf_op jit(solution)/shard_map/dot_general | solution.py:703
  233.6 0.1 copy.48
  233.8 0.8 scatter_custom_fusion
  234.6 2.5 %convolution_multiply_fusion = f32[256,3584]{1,0:T(8,128)} fusion(bf16[128,256]{0,1:T(8,128)(2,1)S(1)} %scatter_custom_fusion, bf16[128,3584]{1,0:T(8,128)(2,1)S(1)} %copy-done.1, f32[]{:T(128)S(6)} %mul.239), kind=kOutput, calls=%fused_computation.2 | convolution fusion | flops 235798528 | bytes 4653060 | tf_op jit(solution)/shard_map/dot_general | solution.py:709
  (19 shorter events, 0.1 us)
Async XLA Ops:
  1.3 1.4 copy-start.10
  7.0 1.2 copy-start
  8.2 1.5 copy-start.2
  9.7 1.1 copy-start.3
  10.9 0.9 copy-start.4
  11.8 0.9 copy-start.5
  138.7 1.7 copy-start.6
  143.4 1.0 copy-start.9
  143.4 1.2 copy-start.7
  151.7 2.1 copy-start.8
  212.4 5.9 %copy-start.1 = (bf16[128,3584]{1,0:T(8,128)(2,1)S(1)}, bf16[128,3584]{1,0:T(8,128)(2,1)}, u32[]{:S(2)}) copy-start(bf16[128,3584]{1,0:T(8,128)(2,1)} %queries.1) | copy-start | bytes 2752516

commit v4 on v3

--- a/solution.py
+++ b/solution.py
@@ -67,6 +67,22 @@
     lax.fori_loop(low, high, run, 0)
 
 
+def slopes_of(logits, positives, label_ids, balance):
+    matched = positives[:, 0:1] == label_ids
+    for index in range(1, positives.shape[1]):
+        matched = matched | (positives[:, index : index + 1] == label_ids)
+    signs = jnp.where(matched, 1.0, -1.0)
+    margin = signs * logits
+    small = jnp.exp(-jnp.abs(margin))
+    larger, smaller = 1.0 / (1.0 + small), small / (1.0 + small)
+    missed = jnp.where(margin >= 0.0, smaller, larger)
+    hit = jnp.where(margin >= 0.0, larger, smaller)
+    softened = jnp.maximum(-margin, 0.0) + jnp.log1p(small)
+    loss = jnp.sum(balance * missed * missed * softened)
+    made = balance * signs * (-(missed * missed) * (2.0 * hit * softened + missed))
+    return made.astype(jnp.bfloat16), loss
+
+
 def spread(groups, members, blocks, group_sem, far_sem, core_sem, relay_sem, arrived):
     group, member = lax.axis_index("dp"), lax.axis_index("mp")
     far = lax.rem(member + 2, members)
@@ -134,26 +150,35 @@
 def project_kernel(
     groups,
     members,
-    states,
-    gain,
+    states_far,
     q_weight,
     key_matrix,
     value_matrix,
-    queries,
-    table,
+    queries_far,
+    table_far,
+    gain,
     positives,
     label_ids,
     kept,
     meta,
-    raw,
+    ids,
+    turns,
+    pooled,
+    base,
     slopes,
     blocks,
+    states,
+    queries,
+    table,
+    raw,
+    pools,
     weights,
     normed,
     part,
     got,
     sums,
     terms,
+    local_sem,
     up_sem,
     down_sem,
     side_sem,
@@ -181,11 +206,26 @@
         peer = lax.rem(group + step, groups)
         pl.semaphore_signal(barrier, inc=1, device_id=(peer, member), device_id_type=MESH)
 
+    held = weights.at[group]
+    fetches = [
+        pltpu.make_async_copy(source, target, local_sem.at[index])
+        for index, (source, target) in enumerate(
+            (
+                (q_weight, held.at[:, pl.ds(0, heads)]),
+                (key_matrix, held.at[:, pl.ds(heads, kv)]),
+                (value_matrix, held.at[:, pl.ds(heads + kv, kv)]),
+                (queries_far, queries),
+                (table_far, table),
+                (states_far, states),
+            )
+        )
+    ]
+    for fetch in fetches:
+        fetch.start()
     each(1, members, greet_member)
     each(1, groups, greet_group)
-    weights[group, :, :heads] = q_weight[...]
-    weights[group, :, heads : heads + kv] = key_matrix[...]
-    weights[group, :, heads + kv :] = value_matrix[...]
+    for fetch in fetches[:3]:
+        fetch.wait()
     pl.semaphore_wait(barrier, groups + members - 2)
 
     def weight_copy(slot, sem, peer):
@@ -274,6 +314,8 @@
                 one(level + step)
 
     travel(0)
+    for fetch in fetches[3:]:
+        fetch.wait()
 
     root = math.sqrt(table.shape[1])
     logits = (
@@ -285,20 +327,7 @@
         )
         / root
     )
-    matched = positives[:, 0:1] == label_ids[...]
-    for index in range(1, positives.shape[1]):
-        matched = matched | (positives[:, index : index + 1] == label_ids[...])
-    signs = jnp.where(matched, 1.0, -1.0)
-    margin = signs * logits
-    small = jnp.exp(-jnp.abs(margin))
-    larger, smaller = 1.0 / (1.0 + small), small / (1.0 + small)
-    missed = jnp.where(margin >= 0.0, smaller, larger)
-    hit = jnp.where(margin >= 0.0, larger, smaller)
-    softened = jnp.maximum(-margin, 0.0) + jnp.log1p(small)
-    loss = jnp.sum(kept[...] * missed * missed * softened)
-    early = (
-        kept[...] * signs * (-(missed * missed) * (2.0 * hit * softened + missed))
-    ).astype(jnp.bfloat16)
+    early, loss = slopes_of(logits, positives[...], label_ids[...], kept[...])
     slopes[...] = early
     for at in range(groups):
         part[at] = (
@@ -338,6 +367,27 @@
             normed[piece, at, :] = ready[:, piece * block : (piece + 1) * block]
 
     each(0, tokens // 64, normalize)
+    texts, length = pooled.shape[0], tokens // pooled.shape[0]
+    chunk, share = tokens // members, texts // members
+
+    def living(index):
+        live = ids[index] != 0
+        row = lax.broadcasted_iota(jnp.int32, (share, chunk), 0)
+        column = lax.broadcasted_iota(jnp.int32, (share, chunk), 1)
+        chosen = jnp.where((lax.div(column, length) == row) & live, 1.0, 0.0)
+        return chosen.astype(jnp.bfloat16), jnp.sum(chosen, axis=1, keepdims=True)
+
+    chosen, counted = living(member)
+    mine = pl.ds(pl.multiple_of(member * chunk, chunk), chunk)
+    for at in range(groups):
+        base[at] = (
+            jnp.dot(
+                chosen,
+                states[mine, at * block : (at + 1) * block],
+                preferred_element_type=jnp.float32,
+            )
+            / counted
+        )
     raw[...] = jnp.zeros_like(raw)
     multiply_step(0)
     travel(1)
@@ -384,6 +434,43 @@
     for step in range(2, depth):
         multiply_across(step)
 
+    def attend_some(index):
+        at = pl.ds(pl.multiple_of(index * chunk, chunk), chunk)
+
+        def rotate(values):
+            turned = pltpu.roll(values, HEAD_WIDTH // 2, 1)
+            return (values * turns[0] + turned * turns[1]).astype(jnp.bfloat16)
+
+        row = lax.broadcasted_iota(jnp.int32, (chunk, chunk), 0)
+        column = lax.broadcasted_iota(jnp.int32, (chunk, chunk), 1)
+        allowed = (lax.div(row, length) == lax.div(column, length)) & (column <= row)
+        allowed = allowed & (ids[index] != 0)
+        chosen, counted = living(index)
+        repeat = heads // kv
+        out = pl.ds(pl.multiple_of(index * share, share), share)
+        for head in range(heads // HEAD_WIDTH):
+            if head % repeat == 0:
+                start = heads + head // repeat * HEAD_WIDTH
+                keys = rotate(raw[at, start : start + HEAD_WIDTH])
+                values = raw[at, start + kv : start + kv + HEAD_WIDTH].astype(jnp.bfloat16)
+            columns = slice(head * HEAD_WIDTH, (head + 1) * HEAD_WIDTH)
+            scores = lax.dot_general(
+                rotate(raw[at, columns]),
+                keys,
+                (((1,), (1,)), ((), ())),
+                preferred_element_type=jnp.float32,
+            ) / math.sqrt(HEAD_WIDTH)
+            made = jnp.where(allowed, jnp.exp(scores), 0.0)
+            probs = (made / jnp.sum(made, axis=1, keepdims=True)).astype(jnp.bfloat16)
+            mixed = jnp.dot(probs, values, preferred_element_type=jnp.float32)
+            pools[out, columns] = (
+                jnp.dot(chosen, mixed.astype(jnp.bfloat16), preferred_element_type=jnp.float32)
+                / counted
+            )
+
+    each(0, members, attend_some)
+    pooled[...] = pools[...].astype(jnp.bfloat16)
+
     each(1, members, lambda step: member_copy(step).wait_send())
     each(1, groups, lambda step: group_copy(step).wait_send())
 
@@ -404,42 +491,54 @@
 
 def project(
     states,
-    gain,
     q_weight,
     key_matrix,
     value_matrix,
     queries,
     table,
+    gain,
     positives,
     label_ids,
     kept,
     meta,
+    ids,
+    turns,
     groups,
     members,
 ):
     tokens, width = states.shape
     batch = queries.shape[0]
+    heads = q_weight.shape[1]
+    texts = members * (meta.shape[0])
     rows, block = batch // members, width // groups
-    columns = q_weight.shape[1] + key_matrix.shape[1] + value_matrix.shape[1]
+    columns = heads + key_matrix.shape[1] + value_matrix.shape[1]
     group_sems = [pltpu.SemaphoreType.DMA((groups,))]
     return pl.pallas_call(
         functools.partial(project_kernel, groups, members),
         out_shape=(
-            jax.ShapeDtypeStruct((tokens, columns), jnp.float32),
+            jax.ShapeDtypeStruct((texts, heads), jnp.bfloat16),
+            jax.ShapeDtypeStruct((groups, texts // members, block), jnp.float32),
             jax.ShapeDtypeStruct((batch, table.shape[0]), jnp.bfloat16),
             jax.ShapeDtypeStruct(
                 (groups * members, rows + meta.shape[0], block), jnp.float32
             ),
         ),
-        in_specs=[pl.BlockSpec(memory_space=pltpu.VMEM)] * 11,
-        out_specs=tuple([pl.BlockSpec(memory_space=pltpu.VMEM)] * 3),
+        in_specs=[pl.BlockSpec(memory_space=pl.ANY)] * 6
+        + [pl.BlockSpec(memory_space=pltpu.VMEM)] * 7,
+        out_specs=tuple([pl.BlockSpec(memory_space=pltpu.VMEM)] * 4),
         scratch_shapes=[
+            pltpu.VMEM(states.shape, jnp.bfloat16),
+            pltpu.VMEM(queries.shape, jnp.bfloat16),
+            pltpu.VMEM(table.shape, jnp.bfloat16),
+            pltpu.VMEM((tokens, columns), jnp.float32),
+            pltpu.VMEM((texts, heads), jnp.float32),
             pltpu.VMEM((groups, block, columns), jnp.bfloat16),
             pltpu.VMEM((groups, tokens, block), jnp.bfloat16),
             pltpu.VMEM((groups, batch, block), jnp.float32),
             pltpu.VMEM((members, groups, rows, block), jnp.float32),
             pltpu.VMEM((groups, rows, block), jnp.float32),
             pltpu.VMEM((groups, rows, block), jnp.float32),
+            pltpu.SemaphoreType.DMA((6,)),
             *(group_sems * 4),
             pltpu.SemaphoreType.DMA((members,)),
             pltpu.SemaphoreType.DMA((members,)),
@@ -452,21 +551,45 @@
         name="project",
     )(
         states,
-        gain,
         q_weight,
         key_matrix,
         value_matrix,
         queries,
         table,
+        gain,
         positives,
         label_ids,
         kept,
         meta,
+        ids,
+        turns,
     )
 
 
 def tail_kernel(
-    groups, members, pooled, weight, base, blocks, pool, terms, parts, s1, r1, s2, r2, *sems
+    groups,
+    members,
+    owned,
+    pooled,
+    weight,
+    base,
+    queries,
+    positives,
+    early,
+    reduced,
+    query_out,
+    slopes,
+    scalars,
+    blocks,
+    pool,
+    terms,
+    parts,
+    rows_wide,
+    s1,
+    r1,
+    s2,
+    r2,
+    *sems,
 ):
     group, member = lax.axis_index("dp"), lax.axis_index("mp")
     own = group * members + member
@@ -533,7 +656,57 @@
     blocks[own] = jnp.concatenate(rows, axis=0).astype(jnp.bfloat16)
     start, end = spread(groups, members, blocks, *sems)
     start()
+    texts = devices * share
+    block = base.shape[2]
+    batch = queries.shape[0]
+    height = batch // members
+    notes = reduced[0, height:, :]
+    for at in range(1, devices):
+        notes = notes + reduced[at, height:, :]
+    new_ids = notes[0:1, :texts].astype(jnp.int32)
+    scalars[...] = notes[:, :128]
     end()
+
+    def widen(at):
+        wide = blocks[at].astype(jnp.float32)
+        for piece in range(groups):
+            rows_wide[piece, pl.ds(pl.multiple_of(at * share, share), share), :] = wide[
+                piece * share : (piece + 1) * share
+            ]
+
+    each(0, devices, widen)
+    root = math.sqrt(groups * block)
+    logits = jnp.zeros((batch, texts), jnp.float32)
+    for piece in range(groups):
+        logits = logits + lax.dot_general(
+            queries[:, piece * block : (piece + 1) * block],
+            rows_wide[piece].astype(jnp.bfloat16),
+            (((1,), (1,)), ((), ())),
+            preferred_element_type=jnp.float32,
+        )
+    late, loss = slopes_of(logits / root, positives[...], new_ids, notes[1:2, :texts])
+    line = lax.broadcasted_iota(jnp.int32, scalars.shape, 0)
+    scalars[...] = scalars[...] + jnp.where(line == 3, loss, 0.0)
+    for piece in range(groups):
+        made = (
+            jnp.dot(
+                late, rows_wide[piece].astype(jnp.bfloat16), preferred_element_type=jnp.float32
+            )
+            / root
+        )
+        for index in range(members):
+            query_out[
+                index * height : (index + 1) * height, piece * block : (piece + 1) * block
+            ] = (
+                made[index * height : (index + 1) * height]
+                + reduced[piece * members + index, :height, :]
+            )
+    labels = own * owned + lax.broadcasted_iota(jnp.int32, (owned, texts), 0)
+    place = jnp.where(labels == new_ids, 1.0, 0.0).astype(jnp.bfloat16)
+    moved = lax.dot_general(
+        late, place, (((1,), (1,)), ((), ())), preferred_element_type=jnp.float32
+    )
+    slopes[...] = (early[...].astype(jnp.float32) + moved).astype(jnp.bfloat16)
     each(1, groups, lambda step: pool_copy(step).wait_send())
 
     def part_sent(step):
@@ -543,20 +716,26 @@
     each(1, devices, part_sent)
 
 
-def tail(pooled, weight, base, groups, members):
+def tail(pooled, weight, base, queries, positives, early, reduced, groups, members):
     texts, heads = pooled.shape
     block = weight.shape[1]
     share = texts // members
     devices = groups * members
     return pl.pallas_call(
-        functools.partial(tail_kernel, groups, members),
-        out_shape=jax.ShapeDtypeStruct((devices, groups * share, block), jnp.bfloat16),
-        in_specs=[pl.BlockSpec(memory_space=pltpu.VMEM)] * 3,
-        out_specs=pl.BlockSpec(memory_space=pltpu.VMEM),
+        functools.partial(tail_kernel, groups, members, early.shape[1]),
+        out_shape=(
+            jax.ShapeDtypeStruct(queries.shape, jnp.float32),
+            jax.ShapeDtypeStruct(early.shape, jnp.bfloat16),
+            jax.ShapeDtypeStruct((8, 128), jnp.float32),
+        ),
+        in_specs=[pl.BlockSpec(memory_space=pltpu.VMEM)] * 7,
+        out_specs=tuple([pl.BlockSpec(memory_space=pltpu.VMEM)] * 3),
         scratch_shapes=[
+            pltpu.VMEM((devices, groups * share, block), jnp.bfloat16),
             pltpu.VMEM((groups, texts, heads), jnp.bfloat16),
             pltpu.VMEM((devices, share, block), jnp.float32),
             pltpu.VMEM((devices, share, block), jnp.float32),
+            pltpu.VMEM((groups, devices * share, block), jnp.float32),
             pltpu.SemaphoreType.DMA((groups,)),
             pltpu.SemaphoreType.DMA((groups,)),
             pltpu.SemaphoreType.DMA((devices,)),
@@ -564,18 +743,125 @@
             *spread_sems(groups, members),
         ],
         compiler_params=pltpu.CompilerParams(
-            collective_id=1, has_side_effects=True, vmem_limit_bytes=24 << 20
+            collective_id=1, has_side_effects=True, vmem_limit_bytes=40 << 20
         ),
         name="tail",
-    )(pooled, weight, base)
+    )(pooled, weight, base, queries, positives, early, reduced)
 
 
 def kernels_fit(groups, members, width, share):
     lanes = -(-(width // groups) // 128) * 128
-    return members == 4 and groups % SIDES == 0 and groups * members * groups * share * lanes * 2 < 8 << 20
+    return (
+        members == 4
+        and share == 8
+        and groups % SIDES == 0
+        and groups * members * share <= width // groups
+        and groups * members * groups * share * lanes * 2 < 8 << 20
+    )
 
 
 def shards(
+    hidden_states,
+    token_ids,
+    norm_gain,
+    q_weight,
+    key_matrix,
+    value_matrix,
+    out_weight,
+    label_table,
+    refresh_rows,
+    label_counts,
+    queries,
+    positives,
+):
+    width = hidden_states.shape[1]
+    texts, length = token_ids.shape
+    groups = lax.axis_size("dp")
+    members = lax.axis_size("mp")
+    share = texts // members
+    if not kernels_fit(groups, members, width, share):
+        return plain_shards(
+            hidden_states,
+            token_ids,
+            norm_gain,
+            q_weight,
+            key_matrix,
+            value_matrix,
+            out_weight,
+            label_table,
+            refresh_rows,
+            label_counts,
+            queries,
+            positives,
+        )
+    block = width // groups
+    root = math.sqrt(width)
+    owned = label_table.shape[0]
+    own = lax.axis_index("dp") * members + lax.axis_index("mp")
+    first_label = own * owned
+    label_ids = first_label + jnp.arange(owned, dtype=jnp.int32)
+    balance = balances(label_counts)
+    replaced = refresh_rows[:, None] == jnp.arange(owned, dtype=jnp.int32)[None, :]
+    kept = jnp.where(jnp.any(replaced, axis=0), 0.0, balance)
+    lanes = jnp.arange(block, dtype=jnp.int32)
+    here = (lanes // share) == own
+    spot = lanes % share
+    picked = (spot[None, :] == jnp.arange(share, dtype=jnp.int32)[:, None]) & here[None, :]
+    new_balance = jnp.sum(jnp.where(replaced, balance[None, :], 0.0), axis=1)
+    new_ids = (first_label + refresh_rows).astype(jnp.float32)
+    meta = jnp.concatenate(
+        [
+            jnp.sum(jnp.where(picked, new_ids[:, None], 0.0), axis=0, keepdims=True),
+            jnp.sum(jnp.where(picked, new_balance[:, None], 0.0), axis=0, keepdims=True),
+            jnp.broadcast_to(jnp.sum(balance), (1, block)),
+            jnp.zeros((5, block), jnp.float32),
+        ],
+        axis=0,
+    )
+    half = HEAD_WIDTH // 2
+    frequency = rope_theta ** (-2.0 * jnp.arange(half, dtype=jnp.float32) / HEAD_WIDTH)
+    places = jnp.arange(share * length, dtype=jnp.int32) % length
+    angles = places.astype(jnp.float32)[:, None] * frequency[None, :]
+    cosine, sine = jnp.cos(angles), jnp.sin(angles)
+    turns = jnp.stack(
+        [
+            jnp.concatenate([cosine, cosine], axis=1),
+            jnp.concatenate([-sine, sine], axis=1),
+        ]
+    )
+    pooled, base, early, reduced = project(
+        hidden_states,
+        q_weight,
+        key_matrix,
+        value_matrix,
+        queries,
+        label_table,
+        norm_gain[None, :],
+        positives,
+        label_ids[None, :],
+        kept[None, :],
+        meta,
+        token_ids.reshape(members, 1, share * length),
+        turns,
+        groups,
+        members,
+    )
+    query_sum, slopes, scalars = tail(
+        pooled, out_weight.T, base, queries, positives, early, reduced, groups, members
+    )
+    total_labels = owned * groups * members
+    factor = total_labels / scalars[2, 0]
+    loss = factor * scalars[3, 0] / (queries.shape[0] * total_labels)
+    label_part = (
+        lax.dot_general(
+            slopes, queries, (((0,), (0,)), ((), ())), preferred_element_type=jnp.float32
+        )
+        / root
+    )
+    return (factor * label_part, factor * query_sum, loss)
+
+
+def plain_shards(
     hidden_states,
     token_ids,
     norm_gain,
@@ -592,75 +878,15 @@
     width = hidden_states.shape[1]
     group_tokens = hidden_states.shape[0]
     texts, length = token_ids.shape
-    groups = lax.axis_size("dp")
-    members = lax.axis_size("mp")
-    share = texts // members
-    member = lax.axis_index("mp")
+    states = hidden_states.astype(jnp.float32)
+    scaled = lax.rsqrt(jnp.mean(states * states, axis=1, keepdims=True) + norm_eps)
+    normed = (states * scaled * norm_gain).astype(jnp.bfloat16)
     heads = q_weight.shape[1]
     kv = key_matrix.shape[1]
-    block = width // groups
-    use_kernels = kernels_fit(groups, members, width, share)
-    root = math.sqrt(width)
-    owned = label_table.shape[0]
-    first_label = (lax.axis_index("dp") * members + member) * owned
-    label_ids = first_label + jnp.arange(owned, dtype=jnp.int32)
-    balance = balances(label_counts)
-    replaced = jnp.any(
-        refresh_rows[:, None] == jnp.arange(owned, dtype=jnp.int32)[None, :], axis=0
-    )
-    kept = jnp.where(replaced, 0.0, balance)
-    new_ids = first_label + refresh_rows
-    new_balance = balances(label_counts[refresh_rows])
-    if use_kernels:
-        sums = jnp.broadcast_to(jnp.sum(balance), (share,))
-        meta = jnp.pad(
-            jnp.stack([new_ids.astype(jnp.float32), new_balance, sums]),
-            ((0, 5), (0, block - share)),
-        )
-        raw, early_slopes, reduced = project(
-            hidden_states,
-            norm_gain[None, :],
-            q_weight,
-            key_matrix,
-            value_matrix,
-            queries,
-            label_table,
-            positives,
-            label_ids[None, :],
-            kept[None, :],
-            meta,
-            groups,
-            members,
-        )
-        rows = queries.shape[0] // members
-        query_sum = (
-            reduced[:, :rows]
-            .reshape(groups, members, rows, block)
-            .transpose(1, 2, 0, 3)
-            .reshape(queries.shape[0], width)
-        )
-        new_ids = reduced[:, rows, :share].reshape(-1).astype(jnp.int32)
-        new_balance = reduced[:, rows + 1, :share].reshape(-1)
-        summed_weight = jnp.sum(reduced[:, rows + 2, 0])
-        loss_sum = jnp.sum(reduced[:, rows + 3, 0])
-    else:
-        states = hidden_states.astype(jnp.float32)
-        scaled = lax.rsqrt(jnp.mean(states * states, axis=1, keepdims=True) + norm_eps)
-        normed = (states * scaled * norm_gain).astype(jnp.bfloat16)
-        weights = lax.all_gather(
-            jnp.concatenate([q_weight, key_matrix, value_matrix], axis=1),
-            "dp",
-            axis=0,
-            tiled=True,
-        )
-        raw = jnp.dot(normed, weights, preferred_element_type=jnp.float32)
-        early_slopes, early_loss = focal(queries, label_table, positives, label_ids, kept, root)
-        query_part = jnp.dot(early_slopes, label_table, preferred_element_type=jnp.float32) / root
-        query_sum, loss_sum, summed_weight = lax.psum(
-            (query_part, early_loss, jnp.sum(balance)), ("dp", "mp")
-        )
-        new_ids = lax.all_gather(new_ids, ("dp", "mp"), axis=0, tiled=True)
-        new_balance = lax.all_gather(new_balance, ("dp", "mp"), axis=0, tiled=True)
+    weights = lax.all_gather(
+        jnp.concatenate([q_weight, key_matrix, value_matrix], axis=1), "dp", axis=0, tiled=True
+    )
+    raw = jnp.dot(normed, weights, preferred_element_type=jnp.float32)
     query_raw = raw[:, :heads]
     key_raw = raw[:, heads : heads + kv]
     value_raw = raw[:, heads + kv :]
@@ -682,6 +908,10 @@
         jnp.sum(attended.astype(jnp.float32).reshape(texts, length, -1) * live[:, :, None], axis=1)
         / counted
     ).astype(jnp.bfloat16)
+    groups = lax.axis_size("dp")
+    members = lax.axis_size("mp")
+    share = texts // members
+    member = lax.axis_index("mp")
     live_own = lax.dynamic_slice_in_dim(live, member * share, share, 0)
     states_own = lax.dynamic_slice_in_dim(
         hidden_states, member * share * length, share * length, 0
@@ -690,44 +920,49 @@
     base_own = (
         jnp.sum(states_own.astype(jnp.float32) * live_own[:, :, None], axis=1) / counted_own
     )
-    if use_kernels:
-        base_blocks = jnp.swapaxes(base_own.reshape(share, groups, block), 0, 1)
-        gathered = tail(pooled, out_weight.T, base_blocks, groups, members)
-        refreshed_all = jnp.swapaxes(
-            gathered.reshape(groups * members, groups, share, block), 1, 2
-        ).reshape(groups * members * share, width)
-    else:
-        refreshed_all = gather_refreshed(pooled, out_weight, base_own, groups, members)
-
-    late_slopes, late_loss = focal(queries, refreshed_all, positives, new_ids, new_balance, root)
-    query_late = jnp.dot(late_slopes, refreshed_all, preferred_element_type=jnp.float32) / root
-    own_late = lax.dynamic_slice_in_dim(
-        late_slopes, (lax.axis_index("dp") * members + member) * share, share, 1
-    )
-    slopes = early_slopes.at[:, refresh_rows].set(own_late)
-    label_part = (
-        lax.dot_general(
-            slopes, queries, (((0,), (0,)), ((), ())), preferred_element_type=jnp.float32
-        )
-        / root
-    )
-    total_labels = owned * groups * members
-    factor = total_labels / summed_weight
-    loss = factor * (loss_sum + late_loss) / (queries.shape[0] * total_labels)
-    return (factor * label_part, factor * (query_sum + query_late), loss)
-
-
-def gather_refreshed(pooled, out_weight, base_own, groups, members):
-    share, width = base_own.shape
     pooled_all = lax.all_gather(pooled, "dp", axis=0, tiled=True)
     terms = lax.dot_general(
         pooled_all, out_weight, (((1,), (1,)), ((), ())), preferred_element_type=jnp.float32
     ).reshape(groups, members, share, -1)
     mine = lax.psum_scatter(terms, "mp", scatter_dimension=1, tiled=True)
-    swapped = lax.all_to_all(mine.reshape(groups, share, -1), "dp", 0, 0, tiled=True)
+    mine = mine.reshape(groups, share, -1)
+    swapped = lax.all_to_all(mine, "dp", 0, 0, tiled=True)
     projected = jnp.swapaxes(swapped, 0, 1).reshape(share, width)
     refreshed = (base_own + projected).astype(jnp.bfloat16)
-    return lax.all_gather(refreshed, ("dp", "mp"), axis=0, tiled=True)
+
+    root = math.sqrt(width)
+    owned = label_table.shape[0]
+    first_label = (lax.axis_index("dp") * members + member) * owned
+    label_ids = first_label + jnp.arange(owned, dtype=jnp.int32)
+    balance = balances(label_counts)
+    replaced = jnp.any(
+        refresh_rows[:, None] == jnp.arange(owned, dtype=jnp.int32)[None, :], axis=0
+    )
+    kept = jnp.where(replaced, 0.0, balance)
+    early_slopes, early_loss = focal(queries, label_table, positives, label_ids, kept, root)
+    query_part = jnp.dot(early_slopes, label_table, preferred_element_type=jnp.float32) / root
+    query_sum, loss_sum, summed_weight = lax.psum(
+        (query_part, early_loss, jnp.sum(balance)), ("dp", "mp")
+    )
+    new_ids = lax.all_gather(first_label + refresh_rows, ("dp", "mp"), axis=0, tiled=True)
+    new_balance = lax.all_gather(balance[refresh_rows], ("dp", "mp"), axis=0, tiled=True)
+    refreshed_all = lax.all_gather(refreshed, ("dp", "mp"), axis=0, tiled=True)
+    late_slopes, late_loss = focal(queries, refreshed_all, positives, new_ids, new_balance, root)
+    query_late = jnp.dot(late_slopes, refreshed_all, preferred_element_type=jnp.float32) / root
+    own_late = lax.dynamic_slice_in_dim(
+        late_slopes, (lax.axis_index("dp") * members + member) * share, share, 1
+    )
+    slopes = early_slopes.at[:, refresh_rows].set(own_late)
+    label_part = (
+        lax.dot_general(
+            slopes, queries, (((0,), (0,)), ((), ())), preferred_element_type=jnp.float32
+        )
+        / root
+    )
+    total_labels = owned * groups * members
+    factor = total_labels / summed_weight
+    loss = factor * (loss_sum + late_loss) / (queries.shape[0] * total_labels)
+    return (factor * label_part, factor * (query_sum + query_late), loss)
 
 
 def balances(label_counts):

time: 239 us -> 206 us (0.86)
  local copies, waits for them, and re-layouts: 29.2 us -> 9.62 us
  matrix products: 16 us -> 2.49 us
  Pallas kernels: 178 us -> 183 us
  other arithmetic: 11.3 us -> 7.18 us
    dot_general x4 -> x0, matrix products: 13.6 us -> none  [the longest x1 4.82 us: attend(): jnp.einsum('ntgrd,nsgd->ngrts', query_r, key_r, preferred_element_type=jn...]
    reshape x4 -> x1, local copies, waits for them, and re-layouts: 7.86 us -> 0.08 us  [shards(): token_ids.reshape(members, 1, share * length)]
    slice x5 -> x1, local copies, waits for them, and re-layouts: 5.62 us -> 0.52 us  [shards(): loss = factor * scalars[3, 0] / (queries.shape[0] * total_labels)]
    pallas_call x1, Pallas kernels: 121 us -> 124 us  [project(): pl.pallas_call(functools.partial(project_kernel, groups, members), out_sh...]
    another operation x2 -> x0, local copies, waits for them, and re-layouts: 2.71 us -> none
    reduce_sum x5 -> x3, other arithmetic: 4.67 us -> 2.23 us  [the longest x1 1.31 us: shards(): jnp.sum(balance)]
    unnamed x24 -> x17, local copies, waits for them, and re-layouts: 8 us -> 7.5 us
where the time goes in v4:
time: 206 us
  Pallas kernels  183 us (89%)
  local copies, waits for them, and re-layouts  9.62 us (5%)
  other arithmetic  7.18 us (3%)
  between operations  3.26 us (2%)
  matrix products  2.49 us (1%)
    pallas_call x1, Pallas kernels, project(): pl.pallas_call(functools.partial(project_kernel, groups, members), out_sh...  124 us
    pallas_call x1, Pallas kernels, tail(): pl.pallas_call(functools.partial(tail_kernel, groups, members, early.shap...  59 us
    unnamed x17, local copies, waits for them, and re-layouts  7.5 us

profile of v4, /device:TPU:0, one launch (start us, length us, event | category | flops | bytes accessed | tf_op | source)
XLA Modules:
  0.0 205.9 jit_solution(13848208705501441501)
XLA Ops:
  0.6 0.0 copy-start
  0.6 0.0 copy-start.6
  0.7 0.0 copy-start.5
  0.7 0.0 copy-start.4
  0.7 0.8 add_convert_fusion
  1.5 0.7 fusion.2
  2.2 0.1 pad.9.clone
  2.3 1.3 fusion.10
  3.6 0.8 select_reduce_fusion.2
  4.5 0.7 pad.8.clone
  5.2 0.1 select_reduce_fusion.1
  5.3 0.1 maximum_maximum_fusion.meta
  5.4 0.7 broadcast_in_dim.63.gain
  6.1 0.8 copy.24
  6.9 0.1 reshape.60
  7.0 0.8 copy.25.positives
  7.7 0.3 multiply_cosine_fusion
  8.1 0.1 maximum_bitcast_fusion
  8.2 1.5 copy.27
  9.7 0.0 copy-done
  9.7 0.0 copy-done.6
  9.7 0.0 copy-done.5
  9.7 0.0 copy-done.4
  9.7 0.0 copy-start.2
  9.7 1.5 copy-done.2
  11.2 124.4 %project.1 = (bf16[32,896]{1,0:T(8,128)(2,1)S(1)}, f32[8,8,448]{2,1,0:T(8,128)S(1)}, bf16[128,256]{1,0:T(8,128)(2,1)S(1)}, f32[32,40,448]{2,1,0:T(8,128)}) custom-call(bf16[512,3584]{1,0:T(8,128)(2,1)} %states_far.1, bf16[448,896]{1,0:T(8,128)(2,1)S(1)} %copy-done.4, bf16[448,128]{1,0:T(8,128)(2,1)S(1)} %copy-done.5, bf16[448,128]{1,0:T(8,128)(2,1)S(1)} %copy-done.6, ...), custom_call_target="tpu_custom_call" | custom-call | tf_op jit(solution)/shard_map/project/pallas_call | solution.py:516
  135.6 0.0 copy-start.1
  135.6 1.7 copy-done.1
  137.3 59.0 %tail.1 = (f32[128,3584]{1,0:T(8,128)S(1)}, bf16[128,256]{1,0:T(8,128)(2,1)S(1)}, f32[8,128]{1,0:T(8,128)S(1)}) custom-call(bf16[32,896]{1,0:T(8,128)(2,1)S(1)} %get-tuple-element.10.pooled, bf16[896,448]{1,0:T(8,128)(2,1)S(1)} %bitcast.14, f32[8,8,448]{2,1,0:T(8,128)S(1)} %get-tuple-element.11.base, bf16[128,3584]{1,0:T(8,128)(2,1)S(1)} %copy-done, ...), custom_call_target="tpu_custom_call" | custom-call | tf_op jit(solution)/shard_map/tail/pallas_call | solution.py:724
  196.3 0.0 copy-start.3
  196.3 1.2 copy-done.3
  197.5 0.5 fusion.11
  199.4 2.9 %broadcast_multiply_fusion = f32[128,3584]{1,0:T(8,128)} fusion(f32[128,3584]{1,0:T(8,128)} %copy-done.3, f32[]{:T(128)} %bitcast.7), kind=kLoop, calls=%fused_computation.1 | loop fusion | flops 458752 | bytes 3670020 | tf_op jit(solution)/shard_map/mul | solution.py:861
  202.3 2.5 %convolution_multiply_fusion = f32[256,3584]{1,0:T(8,128)} fusion(bf16[128,256]{1,0:T(8,128)(2,1)S(1)} %get-tuple-element.14, bf16[128,3584]{1,0:T(8,128)(2,1)S(1)} %copy-done, f32[]{:T(128)S(6)} %mul.70), kind=kOutput, calls=%fused_computation | convolution fusion | flops 235798528 | bytes 4653060 | tf_op jit(solution)/shard_map/dot_general | solution.py:856
  (8 shorter events, 0.0 us)
Async XLA Ops:
  0.6 9.0 %copy-start = (bf16[128,3584]{1,0:T(8,128)(2,1)S(1)}, bf16[128,3584]{1,0:T(8,128)(2,1)}, u32[]{:S(2)}) copy-start(bf16[128,3584]{1,0:T(8,128)(2,1)} %queries.1) | copy-start | bytes 2752516
  0.6 9.0 %copy-start.6 = (bf16[448,128]{1,0:T(8,128)(2,1)S(1)}, bf16[448,128]{1,0:T(8,128)(2,1)}, u32[]{:S(2)}) copy-start(bf16[448,128]{1,0:T(8,128)(2,1)} %value_matrix.1) | copy-start | bytes 344068
  0.7 9.0 %copy-start.5 = (bf16[448,128]{1,0:T(8,128)(2,1)S(1)}, bf16[448,128]{1,0:T(8,128)(2,1)}, u32[]{:S(2)}) copy-start(bf16[448,128]{1,0:T(8,128)(2,1)} %key_matrix.1) | copy-start | bytes 344068
  0.7 9.0 %copy-start.4 = (bf16[448,896]{1,0:T(8,128)(2,1)S(1)}, bf16[448,896]{1,0:T(8,128)(2,1)}, u32[]{:S(2)}) copy-start(bf16[448,896]{1,0:T(8,128)(2,1)} %q_weight.1) | copy-start | bytes 2408452
  9.7 1.5 copy-start.2
  135.6 1.7 copy-start.1
  196.3 1.2 copy-start.3

commit v5 on v4

--- a/solution.py
+++ b/solution.py
@@ -179,6 +179,7 @@
     sums,
     terms,
     local_sem,
+    short_sem,
     up_sem,
     down_sem,
     side_sem,
@@ -239,8 +240,35 @@
     def down(slot):
         return weight_copy(slot, down_sem, group - SIDES)
 
-    def across(slot):
-        return weight_copy(slot, side_sem, level * SIDES + 1 - side)
+    partner = level + 1 - 2 * lax.rem(level, 2)
+    middle = block // 32 * 16
+
+    def across(at, from_side, act):
+        slot = at * SIDES + from_side
+        peer = level * SIDES + 1 - side
+
+        @pl.when(at != partner)
+        def _():
+            act(weight_copy(slot, side_sem, peer))
+
+        @pl.when(at == partner)
+        def _():
+            rest = weights.at[slot, pl.ds(middle, block - middle), :]
+            act(remote(rest, rest, side_sem.at[slot], landed.at[slot], (peer, member)))
+
+    def shortcut(at):
+        first = weights.at[at * SIDES + 1 - side, pl.ds(0, middle), :]
+        peer = partner * SIDES + side
+        return remote(first, first, short_sem.at[0], short_sem.at[1], (peer, member))
+
+    def begin(copy):
+        copy.start()
+
+    def arrive(copy):
+        copy.wait_recv()
+
+    def leave(copy):
+        copy.wait_send()
 
     def travel(step):
         @pl.when(level >= step)
@@ -253,7 +281,7 @@
             def _():
                 up(slot).start()
 
-            across(slot).start()
+            across(level - step, side, begin)
 
         if step == 0:
 
@@ -272,7 +300,7 @@
                 def _():
                     down(slot).start()
 
-                across(slot).start()
+                across(level + step, side, begin)
 
     tokens = states.shape[0]
     tile = 128 if tokens % 128 == 0 else tokens
@@ -299,9 +327,15 @@
 
     def multiply_across(step):
         def one(at):
-            slot = at * SIDES + 1 - side
-            across(slot).wait_recv()
-            multiply(slot)
+            if step > 0:
+                across(at, 1 - side, arrive)
+            if step == 1:
+
+                @pl.when(at == partner)
+                def _():
+                    shortcut(at).wait_recv()
+
+            multiply(at * SIDES + 1 - side)
 
         @pl.when(level >= step)
         def _():
@@ -391,6 +425,8 @@
     raw[...] = jnp.zeros_like(raw)
     multiply_step(0)
     travel(1)
+    across(level, 1 - side, arrive)
+    shortcut(level).start()
     each(1, members, member_wait)
     first = pl.multiple_of(member * rows, rows)
 
@@ -476,7 +512,7 @@
 
     def weights_sent(at):
         slot = at * SIDES + side
-        across(slot).wait_send()
+        across(at, side, leave)
 
         @pl.when((at <= level) & (level < depth - 1))
         def _():
@@ -487,6 +523,7 @@
             down(slot).wait_send()
 
     each(0, depth, weights_sent)
+    shortcut(level).wait_send()
 
 
 def project(
@@ -539,6 +576,7 @@
             pltpu.VMEM((groups, rows, block), jnp.float32),
             pltpu.VMEM((groups, rows, block), jnp.float32),
             pltpu.SemaphoreType.DMA((6,)),
+            pltpu.SemaphoreType.DMA((2,)),
             *(group_sems * 4),
             pltpu.SemaphoreType.DMA((members,)),
             pltpu.SemaphoreType.DMA((members,)),
@@ -754,7 +792,7 @@
     return (
         members == 4
         and share == 8
-        and groups % SIDES == 0
+        and groups % (2 * SIDES) == 0
         and groups * members * share <= width // groups
         and groups * members * groups * share * lanes * 2 < 8 << 20
     )

time: 206 us -> 211 us (1.024)
  Pallas kernels: 183 us -> 187 us
    pallas_call x1, Pallas kernels: 124 us -> 135 us  [project(): pl.pallas_call(functools.partial(project_kernel, groups, members), out_sh...]
    pallas_call x1, Pallas kernels: 59 us -> 52.5 us  [tail(): pl.pallas_call(functools.partial(tail_kernel, groups, members, early.shap...]
where the time goes in v5:
time: 211 us; the launch traced here: 210 us
  Pallas kernels  187 us (89%)
  local copies, waits for them, and re-layouts  9.62 us (5%)
  other arithmetic  7.18 us (3%)
  between operations  3.26 us (2%)
  matrix products  2.49 us (1%)
    pallas_call x1, Pallas kernels, project(): pl.pallas_call(functools.partial(project_kernel, groups, members), out_sh...  135 us
    pallas_call x1, Pallas kernels, tail(): pl.pallas_call(functools.partial(tail_kernel, groups, members, early.shap...  52.5 us
    unnamed x17, local copies, waits for them, and re-layouts  7.5 us

profile of v5, /device:TPU:0, one launch (start us, length us, event | category | flops | bytes accessed | tf_op | source)
XLA Modules:
  0.0 209.8 jit_solution(3627355129775708734)
XLA Ops:
  0.6 0.0 copy-start
  0.6 0.0 copy-start.6
  0.7 0.0 copy-start.5
  0.7 0.0 copy-start.4
  0.7 0.8 add_convert_fusion
  1.5 0.7 fusion.2
  2.2 0.1 pad.9.clone
  2.3 1.3 fusion.10
  3.6 0.8 select_reduce_fusion.2
  4.5 0.7 pad.8.clone
  5.2 0.1 select_reduce_fusion.1
  5.3 0.1 maximum_maximum_fusion.meta
  5.4 0.7 broadcast_in_dim.63.gain
  6.1 0.8 copy.24
  6.9 0.1 reshape.60
  7.0 0.8 copy.25.positives
  7.7 0.3 multiply_cosine_fusion
  8.1 0.1 maximum_bitcast_fusion
  8.2 1.5 copy.27
  9.7 0.0 copy-done
  9.7 0.0 copy-done.6
  9.7 0.0 copy-done.5
  9.7 0.0 copy-done.4
  9.7 0.0 copy-start.2
  9.7 1.5 copy-done.2
  11.2 134.8 %project.1 = (bf16[32,896]{1,0:T(8,128)(2,1)S(1)}, f32[8,8,448]{2,1,0:T(8,128)S(1)}, bf16[128,256]{1,0:T(8,128)(2,1)S(1)}, f32[32,40,448]{2,1,0:T(8,128)}) custom-call(bf16[512,3584]{1,0:T(8,128)(2,1)} %states_far.1, bf16[448,896]{1,0:T(8,128)(2,1)S(1)} %copy-done.4, bf16[448,128]{1,0:T(8,128)(2,1)S(1)} %copy-done.5, bf16[448,128]{1,0:T(8,128)(2,1)S(1)} %copy-done.6, ...), custom_call_target="tpu_custom_call" | custom-call | tf_op jit(solution)/shard_map/project/pallas_call | solution.py:553
  146.0 0.0 copy-start.1
  146.0 1.7 copy-done.1
  147.8 52.5 %tail.1 = (f32[128,3584]{1,0:T(8,128)S(1)}, bf16[128,256]{1,0:T(8,128)(2,1)S(1)}, f32[8,128]{1,0:T(8,128)S(1)}) custom-call(bf16[32,896]{1,0:T(8,128)(2,1)S(1)} %get-tuple-element.10.pooled, bf16[896,448]{1,0:T(8,128)(2,1)S(1)} %bitcast.14, f32[8,8,448]{2,1,0:T(8,128)S(1)} %get-tuple-element.11.base, bf16[128,3584]{1,0:T(8,128)(2,1)S(1)} %copy-done, ...), custom_call_target="tpu_custom_call" | custom-call | tf_op jit(solution)/shard_map/tail/pallas_call | solution.py:762
  200.2 0.0 copy-start.3
  200.3 1.2 copy-done.3
  201.5 0.5 fusion.11
  203.3 2.9 %broadcast_multiply_fusion = f32[128,3584]{1,0:T(8,128)} fusion(f32[128,3584]{1,0:T(8,128)} %copy-done.3, f32[]{:T(128)} %bitcast.7), kind=kLoop, calls=%fused_computation.1 | loop fusion | flops 458752 | bytes 3670020 | tf_op jit(solution)/shard_map/mul | solution.py:899
  206.2 2.5 %convolution_multiply_fusion = f32[256,3584]{1,0:T(8,128)} fusion(bf16[128,256]{1,0:T(8,128)(2,1)S(1)} %get-tuple-element.14, bf16[128,3584]{1,0:T(8,128)(2,1)S(1)} %copy-done, f32[]{:T(128)S(6)} %mul.70), kind=kOutput, calls=%fused_computation | convolution fusion | flops 235798528 | bytes 4653060 | tf_op jit(solution)/shard_map/dot_general | solution.py:894
  (8 shorter events, 0.0 us)
Async XLA Ops:
  0.6 9.0 %copy-start = (bf16[128,3584]{1,0:T(8,128)(2,1)S(1)}, bf16[128,3584]{1,0:T(8,128)(2,1)}, u32[]{:S(2)}) copy-start(bf16[128,3584]{1,0:T(8,128)(2,1)} %queries.1) | copy-start | bytes 2752516
  0.6 9.0 %copy-start.6 = (bf16[448,128]{1,0:T(8,128)(2,1)S(1)}, bf16[448,128]{1,0:T(8,128)(2,1)}, u32[]{:S(2)}) copy-start(bf16[448,128]{1,0:T(8,128)(2,1)} %value_matrix.1) | copy-start | bytes 344068
  0.7 9.0 %copy-start.5 = (bf16[448,128]{1,0:T(8,128)(2,1)S(1)}, bf16[448,128]{1,0:T(8,128)(2,1)}, u32[]{:S(2)}) copy-start(bf16[448,128]{1,0:T(8,128)(2,1)} %key_matrix.1) | copy-start | bytes 344068
  0.7 9.0 %copy-start.4 = (bf16[448,896]{1,0:T(8,128)(2,1)S(1)}, bf16[448,896]{1,0:T(8,128)(2,1)}, u32[]{:S(2)}) copy-start(bf16[448,896]{1,0:T(8,128)(2,1)} %q_weight.1) | copy-start | bytes 2408452
  9.7 1.5 copy-start.2
  146.0 1.7 copy-start.1
  200.2 1.2 copy-start.3
